TPU v7x, 256 devices: a whole 4x4x8 slice. The times are simulated.
256 devices in a mesh: pool: 2 (over core), dev: 128 (over z, y, x).
Axes of the slice: x: 4, y: 4, z: 8, core: 2. Of those that a mesh axis runs over, the one named last changes fastest.
Arguments:
- query_lat: bfloat16 [2, 256, 128, 576], P(None, ('pool', 'dev'))
- step_latent: bfloat16 [2, 256, 576], P(None, ('pool', 'dev'))
- resident_cache: bfloat16 [256, 2048, 576], P(('pool', 'dev')), may hold values from -6 to 6
- resident_len: int32 [256], P(('pool', 'dev')), may hold values from 1 to 2048, as said below
- new_pages: bfloat16 [32768, 8, 576], P(('pool', 'dev')), may hold values from -6 to 6
- page_owner: int32 [32768, 1], P(('pool', 'dev')), may hold values from 0 to 127; in each aligned block of 128 rows (0 to 127, 128 to 255, ...) at most 2 rows name the same one
- moe_input: bfloat16 [256, 7168], P(('pool', 'dev')), may hold values from -6 to 6
- expert_ids: int32 [256, 8], P(('pool', 'dev')), may hold values from 0 to 15, all different within a row; in each aligned block of 256 rows (0 to 255, 256 to 511, ...) at most 192 rows name the same one
- gate_weights: bfloat16 [256, 8], P(('pool', 'dev')), may hold values from 0.099609375 to 0.5
- w_in: bfloat16 [256, 7168, 256], P(('pool', 'dev')), may hold values from -0.0625 to 0.0625
- w_out: bfloat16 [256, 128, 7168], P(('pool', 'dev')), may hold values from -0.125 to 0.125
Outputs:
- context: bfloat16 [2, 256, 128, 512], P(None, ('pool', 'dev'))
- mixed: bfloat16 [256, 7168], P(('pool', 'dev'))
Inputs may be any that keep to these rules, and one draw needn't show every extreme that they name: `page_owner`: the 128 pages of one device name one owner at most 2 times; in some device exactly 2. `expert_ids`: each row names 8 different experts; no expert is named by more than 192 rows, a bound that some block reaches. `resident_len`: some request has exactly 2048 rows.
All inputs are finite; a program needn't handle non-finite values.
Results may differ from a plain program's by a relative error of at most 0.0055.
Values may be sent and summed in bfloat16 or wider, within the bound.
No kernel may reach another device: no remote copies, remote signals or barrier semaphores. Data moves between devices by JAX's collectives and lax.ppermute only.
A program may use at most 128 MiB of HBM per device.

v0:
```python
import jax
import jax.numpy as jnp
from jax import lax
from jax.sharding import PartitionSpec as P

ROPE = 64
EXPERTS = 16


SCORE_SCALE = 192.0 ** (-0.5)
MASKED = -1e30


def from_partner(value, axis, bit):
    return lax.ppermute(value, axis, [(i, i ^ 1 << bit) for i in range(lax.axis_size(axis))])


def slot_buffer(pages, owners, peers, slots):
    counted = pages.shape[0]
    target = owners[:, 0]
    hit_table = (target[:, None] == jnp.arange(peers, dtype=jnp.int32)[None, :]).astype(jnp.int32)
    earlier = jnp.cumsum(hit_table, axis=0) - hit_table
    placing = jnp.sum(earlier * hit_table, axis=1)
    slot_key = target * slots + placing
    matched = slot_key[None, :] == jnp.arange(peers * slots, dtype=jnp.int32)[:, None]
    filled = jnp.any(matched, axis=1)
    source = jnp.sum(jnp.where(matched, jnp.arange(counted, dtype=jnp.int32)[None, :], 0), axis=1)
    buffer = jnp.take(pages, source, axis=0).reshape(peers, slots, pages.shape[1], pages.shape[2])
    return (buffer, filled.astype(jnp.int32).reshape(peers, slots))


def attend(query, sources, width):
    scored = []
    for key_rows, live_rows in sources:
        raw = (
            jnp.einsum("hl,kl->hk", query, key_rows, preferred_element_type=jnp.float32)
            * SCORE_SCALE
        )
        scored.append(jnp.where(live_rows[None, :], raw, MASKED))
    highest = jnp.max(scored[0], axis=1)
    for extra in scored[1:]:
        highest = jnp.maximum(highest, jnp.max(extra, axis=1))
    total = jnp.zeros_like(highest)
    context = jnp.zeros((query.shape[0], width), jnp.float32)
    for source_pair, raw in zip(sources, scored):
        weights = jnp.exp(raw - highest[:, None])
        total = total + jnp.sum(weights, axis=1)
        context = context + jnp.einsum(
            "hk,kc->hc",
            weights.astype(jnp.bfloat16),
            source_pair[0][:, :width],
            preferred_element_type=jnp.float32,
        )
    return (context / total[:, None]).astype(jnp.bfloat16)


def local(
    query_lat,
    step_latent,
    resident_cache,
    resident_len,
    new_pages,
    page_owner,
    moe_input,
    expert_ids,
    gate_weights,
    w_in,
    w_out,
):
    peers = lax.axis_size("dev")
    devices = lax.axis_size("pool") * peers
    slots = max(2, 2 * new_pages.shape[0] // peers)
    buffer, filled = slot_buffer(new_pages, page_owner, peers, slots)
    sent_pages, sent_live = (
        lax.all_to_all(buffer, "dev", split_axis=0, concat_axis=0, tiled=True),
        lax.all_to_all(filled, "dev", split_axis=0, concat_axis=0, tiled=True),
    )
    arrived, arrived_live = from_partner((sent_pages, sent_live), "pool", 0)
    page_rows = arrived.shape[2]
    latent = arrived.shape[3]
    width = latent - ROPE
    arrived_keys = arrived.reshape(-1, latent)
    arrived_mask = jnp.repeat(arrived_live.reshape(-1) > 0, page_rows)
    cached = resident_cache[0]
    cached_mask = jnp.arange(cached.shape[0], dtype=jnp.int32) < resident_len[0]
    outputs = []
    for moment in range(2):
        own_keys = step_latent[: moment + 1, 0]
        own_mask = jnp.ones((moment + 1,), bool)
        sources = [(cached, cached_mask), (arrived_keys, arrived_mask), (own_keys, own_mask)]
        outputs.append(attend(query_lat[moment, 0], sources, width))
    context = jnp.stack(outputs)[:, None]
    flat_rows, flat_ids, gathered_gates = (
        lax.all_gather(moe_input, ("pool", "dev"), axis=0, tiled=True),
        lax.all_gather(expert_ids, ("pool", "dev"), axis=0, tiled=True),
        lax.all_gather(gate_weights, ("pool", "dev"), axis=0, tiled=True),
    )
    flat_gates = gathered_gates.astype(jnp.float32)
    slice_index = lax.axis_index("pool") * peers + lax.axis_index("dev")
    group = devices // EXPERTS
    my_expert = slice_index // group
    row_weight = jnp.sum(jnp.where(flat_ids == my_expert, flat_gates, 0.0), axis=1)
    hidden_units = w_out.shape[1]
    both = jnp.dot(flat_rows, w_in[0], preferred_element_type=jnp.float32)
    hidden = (jax.nn.silu(both[:, :hidden_units]) * both[:, hidden_units:]).astype(jnp.bfloat16)
    own_rows = lax.psum_scatter(
        jnp.dot(hidden, w_out[0], preferred_element_type=jnp.float32) * row_weight[:, None],
        ("pool", "dev"),
        scatter_dimension=0,
        tiled=True,
    )
    mixed = own_rows.astype(jnp.bfloat16)
    return (context, mixed)


def solution(mesh):
    in_specs = (
        P(None, ("pool", "dev"), None, None),
        P(None, ("pool", "dev"), None),
        P(("pool", "dev"), None, None),
        P(("pool", "dev")),
        P(("pool", "dev"), None, None),
        P(("pool", "dev"), None),
        P(("pool", "dev"), None),
        P(("pool", "dev"), None),
        P(("pool", "dev"), None),
        P(("pool", "dev"), None, None),
        P(("pool", "dev"), None, None),
    )
    out_specs = (P(None, ("pool", "dev"), None, None), P(("pool", "dev"), None))
    return jax.shard_map(local, mesh=mesh, in_specs=in_specs, out_specs=out_specs, check_vma=False)
```

profile of v0, /device:TPU:24, one launch (start us, length us, event | category | flops | bytes accessed | tf_op | source)
XLA Modules:
  0.0 1635.3 jit_solution(10107260838743567069)
XLA Ops:
  7.2 0.0 copy-start
  7.2 0.9 fusion.81
  8.1 0.2 reduce_window_sum.11
  8.2 0.8 select_reduce_fusion.1
  9.1 0.7 multiply_add_fusion
  9.7 0.1 select_reduce_fusion
  9.8 0.1 reduce_sum.82
  10.0 2.2 copy.22
  12.3 2.4 gather_fusion
  14.7 3.0 broadcast_select_fusion
  17.7 15.5 all-to-all-start.1
  33.3 0.0 all-gather.5.cloned.1.call-start
  33.3 0.7 all-gather.5.cloned.1.call-update
  34.0 0.0 copy-start.8
  34.0 0.0 copy-start.7
  34.0 0.0 copy-start.5
  34.0 61.5 %all-to-all-done.1 = bf16[128,2,8,576]{3,2,1,0:T(8,128)(2,1)} async-done(((bf16[128,2,8,576]{3,2,1,0:T(8,128)(2,1)}), bf16[128,2,8,576]{3,2,1,0:T(8,128)(2,1)}, u32[]{:S(2)}, u32[]{:S(2)}) %all-to-all-start.1) | async-done | bytes 2359328 | tf_op jit(solution)/shard_map/all_to_all | solution.py:75
  95.5 4.7 copy.23
  100.2 0.0 collective-permute-start.1
  100.2 0.1 fusion.71
  100.4 0.8 reshape.113
  101.1 9.2 all-to-all-start
  111.0 0.0 copy-start.1
  111.0 0.0 copy-done.8
  111.1 598.1 %all-gather.1 = s32[256,1,8]{2,1,0:T(1,128)S(1)} all-gather(s32[1,1,8]{2,1,0:T(1,128)S(1)} %bitcast.99), channel_id=1, replica_groups=mesh['pool'=2,'dev'=128] {'pool','dev'}, dimensions={0}, use_global_device_ids=true | all-gather | bytes 8224 | tf_op jit(solution)/shard_map/all_gather | solution.py:95
  709.2 0.0 copy-done.7
  709.2 0.0 copy-done.5
  709.2 0.1 fusion.94
  709.4 3.3 fusion.97
  712.6 0.0 copy-done.1
  712.7 0.7 fusion.95
  713.3 0.0 copy-done.9
  713.3 629.0 %all-gather.2 = bf16[256,1,8]{2,1,0:T(2,128)(2,1)S(1)} all-gather(bf16[1,1,8]{2,1,0:T(2,128)(2,1)S(1)} %bitcast.100), channel_id=1, replica_groups=mesh['pool'=2,'dev'=128] {'pool','dev'}, dimensions={0}, use_global_device_ids=true | all-gather | bytes 4112 | tf_op jit(solution)/shard_map/all_gather | solution.py:96
  1342.4 0.0 all-to-all-done
  1342.4 0.6 copy-done.6
  1343.0 0.0 collective-permute-start
  1343.0 1.0 fusion.72
  1344.0 0.4 collective-permute-done
  1344.5 0.1 gt.13
  1344.6 0.1 broadcast_in_dim.95
  1344.7 0.1 broadcast_in_dim.96
  1344.9 0.0 collective-permute-done.1
  1344.9 5.0 copy.24
  1349.8 2.6 fusion.96
  1352.5 0.3 fusion.54
  1352.8 0.0 copy-done.4
  1352.8 0.0 copy-start.3
  1352.8 0.9 fusion.98
  1353.7 0.1 convert_convert_fusion
  1353.8 0.3 fusion.50
  1354.1 0.0 copy-done.3
  1354.1 0.3 fusion.48
  1354.4 0.3 fusion.52
  1354.8 0.2 fusion.83
  1355.0 0.4 copy-done.2
  1355.4 0.8 fusion.14
  1356.3 0.5 fusion.44
  1356.8 0.8 fusion.12
  1357.6 0.5 fusion.41
  1358.2 0.7 maximum_bitcast_fusion
  1358.9 5.4 fusion
  1364.3 4.1 convolution_multiply_fusion
  1368.4 258.5 %all-reduce.2 = bf16[256,7168]{1,0:T(8,128)(2,1)} all-reduce(f32[256,7168]{1,0:T(8,128)} %convolution_multiply_fusion), channel_id=2, replica_groups=mesh['pool'=2,'dev'=128] {'pool','dev'}, use_global_device_ids=true, to_apply=%region_15.16.clone | all-reduce | flops 1835008 | bytes 11010048
  1627.0 1.5 dynamic-slice_convert_fusion
  (18 shorter events, 0.1 us)
Async XLA Ops:
  7.2 1357.2 %copy-start = (bf16[1,128,7168]{2,1,0:T(8,128)(2,1)S(1)}, bf16[1,128,7168]{2,1,0:T(8,128)(2,1)}, u32[]{:S(2)}) copy-start(bf16[1,128,7168]{2,1,0:T(8,128)(2,1)} %param.21) | copy-start | bytes 5505028
  17.7 77.8 %all-to-all-start.1 = ((bf16[128,2,8,576]{3,2,1,0:T(8,128)(2,1)}), bf16[128,2,8,576]{3,2,1,0:T(8,128)(2,1)}, u32[]{:S(2)}, u32[]{:S(2)}) async-start(bf16[128,2,8,576]{3,2,1,0:T(8,128)(2,1)} %broadcast_select_fusion), calls=%async_computation.1 | async-start | bytes 5242880 | tf_op jit(solution)/shard_map/all_to_all | solution.py:75
  33.3 1325.6 %all-gather.5.cloned.1.call-start = ((), (), s32[]{:S(2)}) async-start(), calls=%async_computation.2 | async-start | bytes 7368704 | tf_op jit(solution)/shard_map/all_gather | solution.py:94
  34.0 77.0 %copy-start.8 = (s32[1,8]{1,0:T(1,128)S(1)}, s32[1,8]{1,0:T(1,128)}, u32[]{:S(2)}) copy-start(s32[1,8]{1,0:T(1,128)} %param.18) | copy-start | bytes 100
  34.0 675.2 %copy-start.7 = (bf16[2,1,576]{2,0,1:T(2,128)(2,1)S(1)}, bf16[2,1,576]{2,0,1:T(2,128)(2,1)}, u32[]{:S(2)}) copy-start(bf16[2,1,576]{2,0,1:T(2,128)(2,1)} %param.12) | copy-start | bytes 6916
  34.0 675.2 %copy-start.5 = (bf16[2,1,128,576]{2,3,1,0:T(8,128)(2,1)S(1)}, bf16[2,1,128,576]{2,3,1,0:T(8,128)(2,1)}, u32[]{:S(2)}) copy-start(bf16[2,1,128,576]{2,3,1,0:T(8,128)(2,1)} %param.11) | copy-start | bytes 884740
  100.2 1244.6 %collective-permute-start.1 = (bf16[128,2,8,576]{0,3,2,1:T(8,128)(2,1)}, bf16[128,2,8,576]{0,3,2,1:T(8,128)(2,1)}, u32[]{:S(2)}, u32[]{:S(2)}) collective-permute-start(bf16[128,2,8,576]{0,3,2,1:T(8,128)(2,1)} %copy.23), channel_id=1, source_target_pairs={{0,128},{128,0},{1,129},{129,1},{2,130},{130,2},{3,131},{131,3},{4... | collective-permute-start | bytes 7077896 | tf_op jit(solution)/shard_map/ppermute | solution.py:15
  101.1 1241.2 %all-to-all-start = ((s32[128,1,2]{2,1,0:T(1,128)}), s32[128,1,2]{2,1,0:T(1,128)S(1)}, u32[]{:S(2)}, u32[]{:S(2)}) async-start(s32[128,1,2]{2,1,0:T(1,128)} %bitcast.4), calls=%async_computation | async-start | bytes 131072 | tf_op jit(solution)/shard_map/all_to_all | solution.py:76
  111.0 601.6 %copy-start.1 = (bf16[1,2048,576]{1,2,0:T(8,128)(2,1)S(1)}, bf16[1,2048,576]{1,2,0:T(8,128)(2,1)}, u32[]{:S(2)}) copy-start(bf16[1,2048,576]{1,2,0:T(8,128)(2,1)} %param.13) | copy-start | bytes 7077892
  712.7 0.7 copy-start.9
  1342.4 0.6 copy-start.6
  1343.0 1.5 collective-permute-start
  1349.8 2.9 copy-start.4
  1352.8 1.3 copy-start.3
  1353.7 1.7 copy-start.2
Sparse Core Ops, SparseCore 0:
  37.7 122.3 all-gather.4
where the time goes:
time: 1640 us
  blocking collectives  1490 us (91%)
  waiting for transfers between devices  62.6 us (4%)
  starting transfers between devices  24.8 us (2%)
  matrix products  20.2 us (1%)
  local copies, waits for them, and re-layouts  18.3 us (1%)
    all_gather x1, blocking collectives, local(): lax.all_gather(gate_weights, ('pool', 'dev'), axis=0, tiled=True)  629 us
    all_gather x1, blocking collectives, local(): lax.all_gather(expert_ids, ('pool', 'dev'), axis=0, tiled=True)  598 us
    unnamed x1, blocking collectives  259 us
    all_to_all x1, waiting for transfers between devices, local(): lax.all_to_all(buffer, 'dev', split_axis=0, concat_axis=0, tiled=True)  61.5 us
  transfers between devices with their start and end apart: 5, of which 2 were waited for; matrix products, arithmetic and copies ran while one was open for 2% of the time, Pallas kernels for 0%

commit v1 on v0

v1 whole, which is shorter than its diff:
```python
import functools
import jax
import jax.numpy as jnp
from jax import lax
from jax.experimental import pallas as pl
from jax.experimental.pallas import tpu as pltpu
from jax.sharding import Mesh, PartitionSpec as P

EXPERTS = 16
SCORE_SCALE = 192.0 ** (-0.5)
MASKED = -1e30
WIDTH = 512
ROPE = 64
SLAB = ("z", "x")
CHIPS = ("z", "y", "x")
EMPTY = 128.0
LANES = 128
FOLD = 8


def swap(value):
    return lax.ppermute(value, "pool", [(0, 1), (1, 0)])


def dot_t(a, b):
    return lax.dot_general(a, b, (((1,), (1,)), ((), ())), preferred_element_type=jnp.float32)


def dot(a, b):
    return jnp.dot(a, b, preferred_element_type=jnp.float32)


def resident_kernel(length_ref, query_ref, own_ref, cache_ref, acc_ref, top_ref, total_ref):
    step = pl.program_id(0)
    rows = cache_ref.shape[1]
    query = query_ref[...]

    @pl.when(step == 0)
    def _():
        own = dot_t(query, own_ref[...]) * SCORE_SCALE
        row = lax.broadcasted_iota(jnp.int32, own.shape, 0)
        col = lax.broadcasted_iota(jnp.int32, own.shape, 1)
        half = own.shape[0] // 2
        live = (col == 0) | ((col == 1) & (row >= half))
        own = jnp.where(live, own, MASKED)
        top = jnp.max(own, axis=1, keepdims=True)
        weights = jnp.exp(own - top)
        top_ref[...] = jnp.broadcast_to(top, top_ref.shape)
        total_ref[...] = jnp.broadcast_to(jnp.sum(weights, axis=1, keepdims=True), total_ref.shape)
        acc_ref[...] = dot(weights.astype(jnp.bfloat16), own_ref[:, :WIDTH])

    keys = cache_ref[...]
    raw = dot(query, keys) * SCORE_SCALE
    place = step * rows + lax.broadcasted_iota(jnp.int32, raw.shape, 1)
    raw = jnp.where(place < length_ref[0], raw, MASKED)
    before = top_ref[:, :1]
    top = jnp.maximum(before, jnp.max(raw, axis=1, keepdims=True))
    scale = jnp.exp(before - top)
    weights = jnp.exp(raw - top)
    total_ref[...] = total_ref[...] * scale + jnp.sum(weights, axis=1, keepdims=True)
    acc_ref[...] = acc_ref[...] * scale + dot_t(weights.astype(jnp.bfloat16), keys[:WIDTH])
    top_ref[...] = jnp.broadcast_to(top, top_ref.shape)


def attend_resident(query, own, cache, length):
    rows, latent = query.shape
    keys = cache.shape[1]
    block = 512
    stat = jax.ShapeDtypeStruct((rows, LANES), jnp.float32)
    return pl.pallas_call(
        resident_kernel,
        grid=(keys // block,),
        in_specs=[
            pl.BlockSpec(memory_space=pltpu.SMEM),
            pl.BlockSpec((rows, latent), lambda i: (0, 0)),
            pl.BlockSpec(own.shape, lambda i: (0, 0)),
            pl.BlockSpec((latent, block), lambda i: (0, i)),
        ],
        out_specs=[
            pl.BlockSpec((rows, WIDTH), lambda i: (0, 0)),
            pl.BlockSpec((rows, LANES), lambda i: (0, 0)),
            pl.BlockSpec((rows, LANES), lambda i: (0, 0)),
        ],
        out_shape=[jax.ShapeDtypeStruct((rows, WIDTH), jnp.float32), stat, stat],
        compiler_params=pltpu.CompilerParams(vmem_limit_bytes=32 * 1024 * 1024),
        cost_estimate=pl.CostEstimate(
            flops=2 * rows * keys * (latent + WIDTH), bytes_accessed=4 * 1024 * 1024, transcendentals=rows * keys
        ),
        name="resident",
    )(length, query, own, cache)


def arrived_kernel(wide_ref, low_ref, high_ref, pages_ref, acc_in_ref, top_in_ref, total_in_ref, out_ref, acc_ref, top_ref, total_ref):
    step = pl.program_id(0)
    rows = out_ref.shape[0]

    @pl.when(step == 0)
    def _():
        acc_ref[...] = acc_in_ref[...]
        top_ref[...] = top_in_ref[...]
        total_ref[...] = total_in_ref[...]

    count = pages_ref.shape[0] * pages_ref.shape[1]
    block = pages_ref[...].reshape(count, pages_ref.shape[2])
    rope = block[:, 2 * WIDTH :]
    scored = []
    for slot, rope_query in ((0, low_ref), (1, high_ref)):
        keys = block[:, slot * WIDTH : (slot + 1) * WIDTH]
        both = dot_t(wide_ref[...], keys)
        raw = (both[:rows] + dot_t(rope_query[...], rope)) * SCORE_SCALE
        raw = jnp.where(both[rows : rows + 1] > EMPTY / 2, MASKED, raw)
        scored.append((keys, raw))
    before = top_ref[:, :1]
    top = before
    for _, raw in scored:
        top = jnp.maximum(top, jnp.max(raw, axis=1, keepdims=True))
    scale = jnp.exp(before - top)
    total = total_ref[...] * scale
    acc = acc_ref[...] * scale
    for keys, raw in scored:
        weights = jnp.exp(raw - top)
        total = total + jnp.sum(weights, axis=1, keepdims=True)
        acc = acc + dot(weights.astype(jnp.bfloat16), keys)
    total_ref[...] = total
    acc_ref[...] = acc
    top_ref[...] = jnp.broadcast_to(top, top_ref.shape)

    @pl.when(step == pl.num_programs(0) - 1)
    def _():
        out_ref[...] = (acc / total[:, :1]).astype(out_ref.dtype)


def attend_arrived(query, pages, partial):
    rows = query.shape[0]
    sources, page, wide = pages.shape
    block = 32
    probe = (lax.broadcasted_iota(jnp.int32, (16, WIDTH), 1) == 0).astype(jnp.bfloat16)
    wide_query = jnp.concatenate([query[:, :WIDTH], probe], axis=0)
    rope = query[:, WIDTH:]
    blank = jnp.zeros_like(rope)
    low = jnp.concatenate([rope, blank], axis=1)
    high = jnp.concatenate([blank, rope], axis=1)
    whole = lambda a: pl.BlockSpec(a.shape, lambda i: (0,) * a.ndim)
    acc, top, total = partial
    keys = 2 * sources * page
    return pl.pallas_call(
        arrived_kernel,
        grid=(sources // block,),
        in_specs=[whole(wide_query), whole(low), whole(high), pl.BlockSpec((block, page, wide), lambda i: (i, 0, 0)), whole(acc), whole(top), whole(total)],
        out_specs=pl.BlockSpec((rows, WIDTH), lambda i: (0, 0)),
        out_shape=jax.ShapeDtypeStruct((rows, WIDTH), jnp.bfloat16),
        scratch_shapes=[
            pltpu.VMEM((rows, WIDTH), jnp.float32),
            pltpu.VMEM((rows, LANES), jnp.float32),
            pltpu.VMEM((rows, LANES), jnp.float32),
        ],
        compiler_params=pltpu.CompilerParams(vmem_limit_bytes=32 * 1024 * 1024),
        cost_estimate=pl.CostEstimate(
            flops=2 * rows * keys * (2 * WIDTH + LANES), bytes_accessed=4 * 1024 * 1024, transcendentals=rows * keys
        ),
        name="arrived",
    )(wide_query, low, high, pages, acc, top, total)


def slots_kernel(owner_ref, pages_ref, out_ref):
    page, latent, count = pages_ref.shape
    owner = jnp.broadcast_to(owner_ref[...].astype(jnp.float32), (count, count))
    earlier = lax.broadcasted_iota(jnp.int32, owner.shape, 0) < lax.broadcasted_iota(jnp.int32, owner.shape, 1)
    same = jnp.where(earlier & (owner == jnp.transpose(owner)), 1.0, 0.0)
    second = jnp.max(same, axis=0, keepdims=True) > 0.5
    block = 256
    for start in range(0, out_ref.shape[0], block):
        row = start + lax.broadcasted_iota(jnp.int32, (block, 2 * count), 0)
        ropes = []
        for slot in range(2):
            peer = jnp.where(second == (slot == 1), owner_ref[...], -1) * page
            picked, filled = None, None
            for j in range(0, page, 2):
                place = jnp.concatenate([peer + j, peer + j + 1], axis=1)
                hit = jnp.where(row == place, 1.0, 0.0)
                values = jnp.concatenate([pages_ref[j], pages_ref[j + 1]], axis=1)
                term = dot_t(hit.astype(jnp.bfloat16), values)
                picked = term if picked is None else picked + term
                filled = hit if filled is None else filled + hit
            picked = jnp.where(jnp.sum(filled, axis=1, keepdims=True) > 0.5, picked, EMPTY)
            out_ref[pl.ds(start, block), slot * WIDTH : (slot + 1) * WIDTH] = picked[:, :WIDTH].astype(jnp.bfloat16)
            ropes.append(picked[:, WIDTH:])
        out_ref[pl.ds(start, block), 2 * WIDTH :] = jnp.concatenate(ropes, axis=1).astype(jnp.bfloat16)


def slot_buffer(pages, owners, peers):
    page, latent, count = pages.shape
    wide = 2 * latent
    return pl.pallas_call(
        slots_kernel,
        out_shape=jax.ShapeDtypeStruct((peers * page, wide), jnp.bfloat16),
        compiler_params=pltpu.CompilerParams(vmem_limit_bytes=32 * 1024 * 1024),
        cost_estimate=pl.CostEstimate(flops=2 * (peers * page) ** 2 * wide, bytes_accessed=4 * 1024 * 1024, transcendentals=0),
        name="slots",
    )(owners, pages).reshape(peers, page, wide)


def token_kernel(input_ref, ids_ref, gates_ref, out_ref):
    copies, rows, wide = out_ref.shape
    part = wide - LANES
    expert = lax.broadcasted_iota(jnp.int32, (1, LANES), 1)
    gates = gates_ref[...].astype(jnp.float32)
    gate = jnp.zeros((1, LANES), jnp.float32)
    for k in range(ids_ref.shape[1]):
        gate = gate + jnp.where(expert == ids_ref[:, k : k + 1], gates[:, k : k + 1], 0.0)
    values = input_ref[...].astype(jnp.float32)
    lines = [jnp.concatenate([values[:, k * part : (k + 1) * part], gate], axis=1) for k in range(rows)]
    out_ref[...] = jnp.broadcast_to(jnp.concatenate(lines, axis=0).astype(jnp.bfloat16)[None], out_ref.shape)


def unfold_kernel(folded_ref, buffer_ref, partial_ref, out_ref, scratch_ref):
    rows, wide = folded_ref.shape[1:]
    part = wide - LANES
    scratch_ref[...] = folded_ref[...].astype(jnp.float32)
    for k in range(rows):
        out_ref[:, k * part : (k + 1) * part] = scratch_ref[:, k, :part].astype(jnp.bfloat16)
    out_ref[:, rows * part :] = scratch_ref[:, 0, part:].astype(jnp.bfloat16)


def fold_kernel(far_ref, after_ref, before_ref, out_ref, scratch_ref):
    rows, fold, part = out_ref.shape
    for k in range(fold):
        columns = slice(k * part, (k + 1) * part)
        term = far_ref[:rows, columns] + after_ref[:, columns].astype(jnp.float32) + before_ref[:, columns].astype(jnp.float32)
        scratch_ref[:, k, :] = term
    out_ref[...] = scratch_ref[...].astype(jnp.bfloat16)


def shift(value, by):
    count = lax.axis_size("y")
    return lax.ppermute(value, "y", [(i, (i + by) % count) for i in range(count)])


def gather_slab(moe_input, expert_ids, gate_weights, beside):
    slab = lax.axis_size("z") * lax.axis_size("x")
    model = moe_input.shape[1]
    wide = model // FOLD + LANES
    sent = pl.pallas_call(
        token_kernel, out_shape=jax.ShapeDtypeStruct((slab, FOLD, wide), jnp.bfloat16), name="token"
    )(moe_input, expert_ids, gate_weights)
    got = lax.all_to_all(sent, SLAB, 0, 0, tiled=True)
    return pl.pallas_call(
        unfold_kernel,
        in_specs=[pl.BlockSpec(memory_space=pltpu.VMEM)] + [pl.BlockSpec(memory_space=pl.ANY)] * 2,
        out_shape=jax.ShapeDtypeStruct((slab, model + LANES), jnp.bfloat16),
        scratch_shapes=[pltpu.VMEM((slab, FOLD, wide), jnp.float32)],
        name="unfold",
    )(got, *beside)


def expert_part(tokens, w_in, w_out, my_expert):
    model = w_in.shape[0]
    own = tokens.shape[0]
    tokens = jnp.concatenate([tokens, swap(tokens)], axis=0)
    experts = lax.broadcasted_iota(jnp.int32, (1, LANES), 1)
    row_weight = jnp.sum(jnp.where(experts == my_expert, tokens[:, model:].astype(jnp.float32), 0.0), axis=1)
    both = dot(tokens[:, :model], w_in)
    units = both.shape[1] // 2
    hidden = (jax.nn.silu(both[:, :units]) * both[:, units:]).astype(jnp.bfloat16)
    sent = (dot(hidden[own:], w_out) * row_weight[own:, None]).astype(jnp.bfloat16)
    got = swap(sent)
    return dot(hidden[:own], w_out) * row_weight[:own, None] + got.astype(jnp.float32)


def experts_sum(slab, before, after, w_in, w_out, my_expert):
    rows = slab.shape[0]
    half = rows // 2
    first, second = shift(before[:half], 1), shift(after[half:], -1)
    near = expert_part(jnp.concatenate([before, after], axis=0), w_in, w_out, my_expert)
    far = expert_part(jnp.concatenate([slab, first, second], axis=0), w_in, w_out, my_expert)
    opposite = far[rows:].astype(jnp.bfloat16)
    top, bottom = shift(opposite[:half], 1), shift(opposite[half:], -1)
    near_before = jnp.concatenate([near[:half], near[half:rows] + bottom.astype(jnp.float32)], axis=0)
    near_after = jnp.concatenate([near[rows : rows + half] + top.astype(jnp.float32), near[rows + half :]], axis=0)
    terms = (far, shift(near_after.astype(jnp.bfloat16), 1), shift(near_before.astype(jnp.bfloat16), -1))
    folded = (rows, FOLD, far.shape[1] // FOLD)
    return pl.pallas_call(
        fold_kernel,
        out_shape=jax.ShapeDtypeStruct(folded, jnp.bfloat16),
        scratch_shapes=[pltpu.VMEM(folded, jnp.float32)],
        name="fold",
    )(*terms)


def pass_kernel(value_ref, beside_ref, out_ref):
    out_ref[...] = value_ref[...]


def after_both(value, beside):
    vmem = pl.BlockSpec(memory_space=pltpu.VMEM)
    return pl.pallas_call(
        pass_kernel,
        in_specs=[vmem, pl.BlockSpec(memory_space=pl.ANY)],
        out_shape=jax.ShapeDtypeStruct(value.shape, value.dtype),
        name="pass",
    )(value, beside)


def local(
    query_lat,
    step_latent,
    resident_cache,
    resident_len,
    new_pages,
    page_owner,
    moe_input,
    expert_ids,
    gate_weights,
    w_in,
    w_out,
):
    depth = lax.axis_size("z")
    plane = lax.axis_size("y") * lax.axis_size("x")
    peers = depth * plane
    steps, _, heads, latent = query_lat.shape
    query = query_lat.reshape(steps * heads, latent)

    with jax.named_scope("pages"):
        turned = jnp.transpose(new_pages, (1, 2, 0))
        buffer = slot_buffer(swap(turned), swap(page_owner.reshape(1, -1)), peers)
        arrived = lax.all_to_all(buffer, CHIPS, 0, 0, tiled=True)

    with jax.named_scope("resident"):
        own = jnp.concatenate([step_latent[:, 0], jnp.zeros((14, latent), jnp.bfloat16)], axis=0)
        partial = attend_resident(query, own, jnp.transpose(resident_cache[0]), resident_len)

    with jax.named_scope("tokens"):
        slab = gather_slab(moe_input, expert_ids, gate_weights, (buffer, partial[0]))
        before, after = shift(slab, 1), shift(slab, -1)

    with jax.named_scope("experts"):
        group = 2 * peers // EXPERTS
        slice_index = (
            lax.axis_index("pool") * peers
            + lax.axis_index("z") * plane
            + lax.axis_index("y") * lax.axis_size("x")
            + lax.axis_index("x")
        )
        rows, model = slab.shape[0], w_out.shape[2]

        def turn(i, _):
            held, _ = lax.optimization_barrier(((slab, before, after), i))
            return experts_sum(*held, w_in[0], w_out[0], slice_index // group)

        blank = jnp.zeros((rows, FOLD, model // FOLD), jnp.bfloat16)
        sums = lax.fori_loop(0, lax.optimization_barrier(jnp.int32(1)), turn, blank)

    with jax.named_scope("sums"):
        ends = lax.all_to_all(after_both(sums, arrived), SLAB, 0, 0, tiled=True)
        mixed = jnp.sum(ends.astype(jnp.float32), axis=0).reshape(1, model).astype(jnp.bfloat16)

    with jax.named_scope("attention"):
        context = attend_arrived(query, arrived, partial)
        context = context.reshape(steps, 1, heads, WIDTH)
    return (context, mixed)


def solution(mesh):
    chips = Mesh(mesh.devices.reshape(2, 8, 4, 4), ("pool", "z", "y", "x"))
    every = ("pool", "z", "y", "x")
    in_specs = (
        P(None, every, None, None),
        P(None, every, None),
        P(every, None, None),
        P(every),
        P(every, None, None),
        P(every, None),
        P(every, None),
        P(every, None),
        P(every, None),
        P(every, None, None),
        P(every, None, None),
    )
    out_specs = (P(None, every, None, None), P(every, None))
    return jax.shard_map(local, mesh=chips, in_specs=in_specs, out_specs=out_specs, check_vma=False)
```

time: 1640 us -> 141 us (0.09)
  blocking collectives: 1490 us -> 0 us
  Pallas kernels: 0 us -> 24.4 us
    all_gather x2 -> x0, blocking collectives: 1230 us -> none  [the longest x1 629 us: local(): lax.all_gather(gate_weights, ('pool', 'dev'), axis=0, tiled=True)]
    unnamed x1 -> x0, blocking collectives: 259 us -> none
    all_to_all x2 -> x3, waiting for transfers between devices: 61.5 us -> 13.3 us  [the longest x1 9.41 us: local(): ends = lax.all_to_all(after_both(sums, arrived), SLAB, 0, 0, tiled=True)]
    ppermute x2 -> x14, waiting for transfers between devices: 0.43 us -> 39.3 us  [the longest x8 36.4 us: shift(): lax.ppermute(value, 'y', [(i, (i + by) % count) for i in range(count)])]
    pallas_call x0 -> x7, Pallas kernels: none -> 24.4 us  [the longest x1 5.72 us: slot_buffer(): pl.pallas_call(slots_kernel, out_shape=jax.ShapeDtypeStruct((peers * page...]
  transfers between devices with their start and end apart: 5 -> 17, of which waited for: 2 -> 9; matrix products, arithmetic and copies ran while one was open for 2% -> 10% of each run, Pallas kernels for 0% -> 13%
where the time goes in v1:
time: 141 us; the launch traced here: 140 us
  waiting for transfers between devices  52.6 us (37%)
  starting transfers between devices  39.5 us (28%)
  Pallas kernels  24.4 us (17%)
  local copies, waits for them, and re-layouts  13.5 us (10%)
  matrix products  4.39 us (3%)
  other arithmetic  4.14 us (3%)
  between operations  1.44 us (1%)
    ppermute x8, waiting for transfers between devices, shift(): lax.ppermute(value, 'y', [(i, (i + by) % count) for i in range(count)])  36.4 us
    all_to_all x1, starting transfers between devices, gather_slab(): got = lax.all_to_all(sent, SLAB, 0, 0, tiled=True)  11.3 us
    all_to_all x1, starting transfers between devices, local(): arrived = lax.all_to_all(buffer, CHIPS, 0, 0, tiled=True)  9.55 us
    ppermute x8, starting transfers between devices, shift(): lax.ppermute(value, 'y', [(i, (i + by) % count) for i in range(count)])  9.54 us
    all_to_all x1, waiting for transfers between devices, local(): ends = lax.all_to_all(after_both(sums, arrived), SLAB, 0, 0, tiled=True)  9.41 us
    unnamed x16, local copies, waits for them, and re-layouts  8.15 us
    all_to_all x1, starting transfers between devices, local(): ends = lax.all_to_all(after_both(sums, arrived), SLAB, 0, 0, tiled=True)  7.73 us
    pallas_call x1, Pallas kernels, slot_buffer(): pl.pallas_call(slots_kernel, out_shape=jax.ShapeDtypeStruct((peers * page...  5.72 us
  transfers between devices with their start and end apart: 17, of which 9 were waited for; matrix products, arithmetic and copies ran while one was open for 10% of the time, Pallas kernels for 13%

profile of v1, /device:TPU:24, one launch (start us, length us, event | category | flops | bytes accessed | tf_op | source)
XLA Modules:
  0.0 140.1 jit_solution(2557821173385444038)
XLA Ops:
  0.6 0.1 collective-permute-start.11
  0.7 1.7 %token_.1 = bf16[32,8,1024]{2,1,0:T(8,128)(2,1)} custom-call(bf16[1,7168]{1,0:T(2,128)(2,1)} %input_ref.1, s32[1,8]{1,0:T(1,128)} %ids_ref.1, bf16[1,8]{1,0:T(2,128)(2,1)} %gates_ref.1), custom_call_target="tpu_custom_call" | custom-call | tf_op jit(solution)/shard_map/tokens/token/pallas_call | solution.py:243
  2.4 11.3 %all-to-all-start.1 = ((bf16[32,8,1024]{2,1,0:T(8,128)(2,1)}), bf16[32,8,1024]{2,1,0:T(8,128)(2,1)S(1)}, u32[]{:S(2)}, u32[]{:S(2)}) async-start(bf16[32,8,1024]{2,1,0:T(8,128)(2,1)} %token_.1), calls=%async_computation.1 | async-start | bytes 1048576 | tf_op jit(solution)/shard_map/tokens/all_to_all | solution.py:246
  13.8 0.3 collective-permute-start.10
  14.1 1.2 copy.13
  15.9 1.7 %copy-done.4 = bf16[1,2048,576]{1,2,0:T(8,128)(2,1)S(1)} copy-done((bf16[1,2048,576]{1,2,0:T(8,128)(2,1)S(1)}, bf16[1,2048,576]{1,2,0:T(8,128)(2,1)}, u32[]{:S(2)}) %copy-start.4) | copy-done | bytes 2359320
  17.6 4.2 %resident.1 = (f32[256,512]{1,0:T(8,128)S(1)}, f32[256,128]{1,0:T(8,128)S(1)}, f32[256,128]{1,0:T(8,128)S(1)}) custom-call(s32[1]{0:T(128)S(6)} %copy.28.length_ref, bf16[256,576]{1,0:T(8,128)(2,1)S(1)} %bitcast.48, bf16[16,576]{1,0:T(8,128)(2,1)S(1)} %concatenate.55.own_ref, bf16[576,2048]{1,0:T(8,128)(2,1)S(1)} %bitcast.51), custom_call_target="tpu_custom_call" | custom-call | flops 1140850688 | bytes 4194304 | tf_op jit(solution)/shard_map/resident/resident/pallas_call | solution.py:70
  21.8 0.8 copy-done.2
  22.6 5.7 %slots.1 = bf16[1024,1152]{1,0:T(8,128)(2,1)} custom-call(s32[1,128]{1,0:T(1,128)S(1)} %collective-permute-done.10.owner_ref, bf16[8,576,128]{2,1,0:T(8,128)(2,1)S(1)} %collective-permute-done.11.pages_ref), custom_call_target="tpu_custom_call" | custom-call | flops 2415919104 | bytes 4194304 | tf_op jit(solution)/shard_map/pages/slots/pallas_call | solution.py:194
  28.3 3.8 %all-to-all-done.1.folded_ref = bf16[32,8,1024]{2,1,0:T(8,128)(2,1)S(1)} async-done(((bf16[32,8,1024]{2,1,0:T(8,128)(2,1)}), bf16[32,8,1024]{2,1,0:T(8,128)(2,1)S(1)}, u32[]{:S(2)}, u32[]{:S(2)}) %all-to-all-start.1) | async-done | bytes 524320 | tf_op jit(solution)/shard_map/tokens/all_to_all | solution.py:246
  32.1 0.8 copy-done.7
  32.9 3.6 %unfold.1 = bf16[32,7296]{1,0:T(8,128)(2,1)} custom-call(bf16[32,8,1024]{2,1,0:T(8,128)(2,1)} %copy-done.7, bf16[128,8,1152]{2,1,0:T(8,128)(2,1)} %bitcast.5.buffer_ref, f32[256,512]{1,0:T(8,128)} %copy-done.2), custom_call_target="tpu_custom_call" | custom-call | tf_op jit(solution)/shard_map/tokens/unfold/pallas_call | solution.py:247
  36.6 0.2 collective-permute-start.12
  36.8 1.8 %collective-permute-start.13 = (bf16[32,7296]{1,0:T(8,128)(2,1)}, bf16[32,7296]{1,0:T(8,128)(2,1)S(1)}, u32[]{:S(2)}, u32[]{:S(2)}) collective-permute-start(bf16[32,7296]{1,0:T(8,128)(2,1)} %unfold.1), channel_id=1, source_target_pairs={{0,12},{4,0},{8,4},{12,8},{1,13},{5,1},{9,5},{13,9},{2,14},{6,2},{... | collective-permute-start | bytes 1400840 | tf_op jit(solution)/shard_map/tokens/ppermute | solution.py:236
  38.6 9.5 %all-to-all-start = ((bf16[128,8,1152]{2,1,0:T(8,128)(2,1)}), bf16[128,8,1152]{2,1,0:T(8,128)(2,1)S(1)}, u32[]{:S(2)}, u32[]{:S(2)}) async-start(bf16[128,8,1152]{2,1,0:T(8,128)(2,1)} %bitcast.5.buffer_ref), calls=%async_computation | async-start | bytes 4718592 | tf_op jit(solution)/shard_map/pages/all_to_all | solution.py:326
  48.2 1.1 collective-permute-done.13
  49.2 0.8 broadcast_in_dim.32
  50.1 62.7 %while.13 = (s32[]{:T(128)}, bf16[32,8,896]{2,1,0:T(8,128)(2,1)}, s32[]{:T(128)}, bf16[32,7296]{1,0:T(8,128)(2,1)}, bf16[32,7296]{1,0:T(8,128)(2,1)}, /*index=5*...) while((s32[]{:T(128)}, bf16[32,8,896]{2,1,0:T(8,128)(2,1)}, ...), condition=%wide.region_3.4_spmd, body=%wide.region_0.3_spmd.sunk | while | flops 1422278528 | bytes 90101552 | solution.py:351
  50.1 1.1 pad_maximum_fusion.9
  51.1 0.1 collective-permute-start
  51.2 1.0 slice.263
  52.2 0.5 collective-permute-start.1
  52.7 1.7 %collective-permute-start.2 = (bf16[16,7296]{1,0:T(8,128)(2,1)S(1)}, bf16[16,7296]{1,0:T(8,128)(2,1)S(1)}, u32[]{:S(2)}, u32[]{:S(2)}) collective-permute-start(bf16[16,7296]{1,0:T(8,128)(2,1)S(1)} %slice.264), channel_id=1, source_target_pairs={{0,12},{4,0},{8,4},{12,8},{1,13},{5,1},{9,5},{13,9},{2,14},{6,2},{... | collective-permute-start | bytes 700424 | tf_op jit(solution)/shard_map/experts/while/body/ppermute | solution.py:236
  54.4 1.1 constant_dynamic-update-slice_fusion.13
  55.5 1.1 constant_dynamic-update-slice_fusion.14
  56.6 10.3 %collective-permute-done.1 = bf16[16,7296]{1,0:T(8,128)(2,1)S(1)} collective-permute-done((bf16[16,7296]{1,0:T(8,128)(2,1)S(1)}, bf16[16,7296]{1,0:T(8,128)(2,1)S(1)}, u32[]{:S(2)}, u32[]{:S(2)}) %collective-permute-start.1) | collective-permute-done | bytes 233504 | tf_op jit(solution)/shard_map/experts/while/body/ppermute | solution.py:236
  66.9 1.1 pad_maximum_fusion.10
  68.0 0.2 collective-permute-start.3
  68.2 0.1 constant_dynamic-update-slice_fusion.15
  68.4 2.2 %collective-permute-done.3 = bf16[64,7296]{1,0:T(8,128)(2,1)S(1)} collective-permute-done((bf16[64,7296]{1,0:T(8,128)(2,1)S(1)}, bf16[64,7296]{1,0:T(8,128)(2,1)S(1)}, u32[]{:S(2)}, u32[]{:S(2)}) %collective-permute-start.3) | collective-permute-done | bytes 933920 | tf_op jit(solution)/shard_map/experts/while/body/ppermute | solution.py:22
  70.6 0.1 constant_dynamic-update-slice_fusion.18
  70.7 0.1 select_reduce_fusion.3
  70.8 0.1 fusion.61
  70.9 0.7 fusion.62
  71.6 0.8 copy-done.5
  72.4 0.4 fusion.64
  72.8 0.2 collective-permute-start.4
  73.0 0.6 fusion.67
  73.7 0.1 fusion.66
  73.8 0.4 fusion.69
  74.2 0.5 collective-permute-start.5
  74.6 0.7 collective-permute-done.4
  75.3 1.8 %fusion.65 = (bf16[64,7168]{1,0:T(8,128)(2,1)S(1)}, f32[64,7168]{1,0:T(8,128)}) fusion(bf16[64,7168]{1,0:T(8,128)(2,1)S(1)} %collective-permute-done.4, f32[64]{0:T(128)S(1)} %get-tuple-element.317, bf16[1,128,7168]{2,1,0:T(8,128)(2,1)S(1)} %copy-done.5, bf16[128,128]{1,0:T(8,128)(2,1)S(1)} %fusion.63), kind=kOutput, calls=%fused_computation.52.clone.1 | convolution fusion | flops 119275520 | bytes 5521920 | tf_op jit(solution)/shard_map/experts/while/body/dot_general | solution.py:30
  77.1 0.1 collective-permute-start.6
  77.2 3.2 %collective-permute-start.7 = (bf16[16,7168]{1,0:T(8,128)(2,1)S(1)}, bf16[16,7168]{1,0:T(8,128)(2,1)S(1)}, u32[]{:S(2)}, u32[]{:S(2)}) collective-permute-start(bf16[16,7168]{1,0:T(8,128)(2,1)S(1)} %get-tuple-element.327), channel_id=1, source_target_pairs={{0,4},{4,8},{8,12},{12,0},{1,5},{5,9},{9,13},{13,1},{2,6},{6,10},{... | collective-permute-start | bytes 688136 | tf_op jit(solution)/shard_map/experts/while/body/ppermute | solution.py:236
  80.5 0.5 fusion.70
  81.0 10.0 %collective-permute-done.6 = bf16[16,7168]{1,0:T(8,128)(2,1)S(1)} collective-permute-done((bf16[16,7168]{1,0:T(8,128)(2,1)S(1)}, bf16[16,7168]{1,0:T(8,128)(2,1)S(1)}, u32[]{:S(2)}, u32[]{:S(2)}) %collective-permute-start.6) | collective-permute-done | bytes 229408 | tf_op jit(solution)/shard_map/experts/while/body/ppermute | solution.py:236
  91.0 0.1 fusion.73
  91.1 0.8 pad_maximum_fusion.11
  91.9 1.6 %collective-permute-start.8 = (bf16[32,7168]{1,0:T(8,128)(2,1)}, bf16[32,7168]{1,0:T(8,128)(2,1)}, u32[]{:S(2)}, u32[]{:S(2)}) collective-permute-start(bf16[32,7168]{1,0:T(8,128)(2,1)} %pad_maximum_fusion.11), channel_id=1, source_target_pairs={{0,4},{4,8},{8,12},{12,0},{1,5},{5,9},{9,13},{13,1},{2,6},{6,10},{... | collective-permute-start | bytes 1376264 | tf_op jit(solution)/shard_map/experts/while/body/ppermute | solution.py:236
  93.5 0.8 pad_maximum_fusion.12
  94.3 0.4 collective-permute-start.9
  94.7 11.5 %collective-permute-done.8.after_ref = bf16[32,7168]{1,0:T(8,128)(2,1)} collective-permute-done((bf16[32,7168]{1,0:T(8,128)(2,1)}, bf16[32,7168]{1,0:T(8,128)(2,1)}, u32[]{:S(2)}, u32[]{:S(2)}) %collective-permute-start.8) | collective-permute-done | bytes 458784 | tf_op jit(solution)/shard_map/experts/while/body/ppermute | solution.py:236
  106.3 3.5 %collective-permute-done.9.before_ref = bf16[32,7168]{1,0:T(8,128)(2,1)} collective-permute-done((bf16[32,7168]{1,0:T(8,128)(2,1)}, bf16[32,7168]{1,0:T(8,128)(2,1)}, u32[]{:S(2)}, u32[]{:S(2)}) %collective-permute-start.9) | collective-permute-done | bytes 458784 | tf_op jit(solution)/shard_map/experts/while/body/ppermute | solution.py:236
  109.8 2.9 %fold.4 = bf16[32,8,896]{2,1,0:T(8,128)(2,1)} custom-call(f32[64,7168]{1,0:T(8,128)} %get-tuple-element.318.far_ref, bf16[32,7168]{1,0:T(8,128)(2,1)} %collective-permute-done.8.after_ref, bf16[32,7168]{1,0:T(8,128)(2,1)} %collective-permute-done.9.before_ref), custom_call_target="tpu_custom_call" | custom-call | tf_op jit(solution)/shard_map/experts/while/body/fold/pallas_call | solution.py:282
  112.7 1.4 %copy-done = bf16[128,8,1152]{2,1,0:T(8,128)(2,1)} copy-done((bf16[128,8,1152]{2,1,0:T(8,128)(2,1)}, bf16[128,8,1152]{2,1,0:T(8,128)(2,1)S(1)}, u32[]{:S(2)}) %copy-start) | copy-done | bytes 2359320
  114.1 1.8 %pass.1 = bf16[32,8,896]{2,1,0:T(8,128)(2,1)} custom-call(bf16[32,8,896]{2,1,0:T(8,128)(2,1)} %get-tuple-element.194.value_ref, bf16[128,8,1152]{2,1,0:T(8,128)(2,1)} %copy-done), custom_call_target="tpu_custom_call" | custom-call | tf_op jit(solution)/shard_map/sums/pass/pallas_call | solution.py:296
  116.0 7.7 %all-to-all-start.2 = ((bf16[32,8,896]{2,1,0:T(8,128)(2,1)}), bf16[32,8,896]{2,1,0:T(8,128)(2,1)S(1)}, u32[]{:S(2)}, u32[]{:S(2)}) async-start(bf16[32,8,896]{2,1,0:T(8,128)(2,1)} %pass.1), calls=%async_computation.2 | async-start | bytes 917504 | tf_op jit(solution)/shard_map/sums/all_to_all | solution.py:354
  123.8 0.1 fusion.31
  123.9 1.7 %copy-done.1 = bf16[128,8,1152]{2,1,0:T(8,128)(2,1)S(1)} copy-done((bf16[128,8,1152]{2,1,0:T(8,128)(2,1)S(1)}, bf16[128,8,1152]{2,1,0:T(8,128)(2,1)}, u32[]{:S(2)}) %copy-start.1) | copy-done | bytes 2359320
  125.6 4.3 %arrived.1 = bf16[256,512]{1,0:T(8,128)(2,1)} custom-call(bf16[272,512]{1,0:T(8,128)(2,1)S(1)} %pad_maximum_fusion.4.wide_ref, bf16[256,128]{1,0:T(8,128)(2,1)S(1)} %get-tuple-element.234.low_ref, bf16[256,128]{1,0:T(8,128)(2,1)S(1)} %get-tuple-element.233.high_ref, bf16[128,8,1152]{2,1,0:T(8,128)(2,1)S(1)} %copy-done.1, f32[256,512]{1,0:T(8,128)S(1)} %copy-done.3, ...), custom_call_target="tpu_custom_call" | custom-call | flops 1207959552 | bytes 4194304 | tf_op jit(solution)/shard_map/attention/arrived/pallas_call | solution.py:146
  129.9 9.4 %all-to-all-done.2 = bf16[32,8,896]{2,1,0:T(8,128)(2,1)S(1)} async-done(((bf16[32,8,896]{2,1,0:T(8,128)(2,1)}), bf16[32,8,896]{2,1,0:T(8,128)(2,1)S(1)}, u32[]{:S(2)}, u32[]{:S(2)}) %all-to-all-start.2) | async-done | bytes 458784 | tf_op jit(solution)/shard_map/sums/all_to_all | solution.py:354
  139.3 0.1 reduce_sum.36
  139.4 0.6 copy.15
  (34 shorter events, 0.3 us)
Async XLA Ops:
  0.6 15.2 %copy-start.8 = (bf16[2,1,576]{2,0,1:T(2,128)(2,1)S(1)}, bf16[2,1,576]{2,0,1:T(2,128)(2,1)}, u32[]{:S(2)}) copy-start(bf16[2,1,576]{2,0,1:T(2,128)(2,1)} %param.14) | copy-start | bytes 6916
  0.6 21.9 %collective-permute-start.11 = (bf16[8,576,128]{2,1,0:T(8,128)(2,1)}, bf16[8,576,128]{2,1,0:T(8,128)(2,1)S(1)}, u32[]{:S(2)}, u32[]{:S(2)}) collective-permute-start(bf16[8,576,128]{2,1,0:T(8,128)(2,1)} %bitcast.55), channel_id=1, source_target_pairs={{0,128},{128,0},{1,129},{129,1},{2,130},{130,2},{3,131},{131,3},{4... | collective-permute-start | bytes 3538952 | tf_op jit(solution)/shard_map/pages/ppermute | solution.py:22
  2.4 29.7 %all-to-all-start.1 = ((bf16[32,8,1024]{2,1,0:T(8,128)(2,1)}), bf16[32,8,1024]{2,1,0:T(8,128)(2,1)S(1)}, u32[]{:S(2)}, u32[]{:S(2)}) async-start(bf16[32,8,1024]{2,1,0:T(8,128)(2,1)} %token_.1), calls=%async_computation.1 | async-start | bytes 1048576 | tf_op jit(solution)/shard_map/tokens/all_to_all | solution.py:246
  13.8 8.8 %collective-permute-start.10 = (s32[1,128]{1,0:T(1,128)}, s32[1,128]{1,0:T(1,128)S(1)}, u32[]{:S(2)}, u32[]{:S(2)}) collective-permute-start(s32[1,128]{1,0:T(1,128)} %bitcast.56), channel_id=1, source_target_pairs={{0,128},{128,0},{1,129},{129,1},{2,130},{130,2},{3,131},{131,3},{4... | collective-permute-start | bytes 1544 | tf_op jit(solution)/shard_map/pages/ppermute | solution.py:22
  15.9 1.7 %copy-start.4 = (bf16[1,2048,576]{1,2,0:T(8,128)(2,1)S(1)}, bf16[1,2048,576]{1,2,0:T(8,128)(2,1)}, u32[]{:S(2)}) copy-start(bf16[1,2048,576]{1,2,0:T(8,128)(2,1)} %param.15) | copy-start | bytes 7077892
  21.8 0.8 copy-start.2
  32.1 0.8 copy-start.7
  36.6 11.6 %collective-permute-start.12 = (bf16[32,7296]{1,0:T(8,128)(2,1)}, bf16[32,7296]{1,0:T(8,128)(2,1)}, u32[]{:S(2)}, u32[]{:S(2)}) collective-permute-start(bf16[32,7296]{1,0:T(8,128)(2,1)} %unfold.1), channel_id=1, source_target_pairs={{0,4},{4,8},{8,12},{12,0},{1,5},{5,9},{9,13},{13,1},{2,6},{6,10},{... | collective-permute-start | bytes 1400840 | tf_op jit(solution)/shard_map/tokens/ppermute | solution.py:236
  36.8 12.4 %collective-permute-start.13 = (bf16[32,7296]{1,0:T(8,128)(2,1)}, bf16[32,7296]{1,0:T(8,128)(2,1)S(1)}, u32[]{:S(2)}, u32[]{:S(2)}) collective-permute-start(bf16[32,7296]{1,0:T(8,128)(2,1)} %unfold.1), channel_id=1, source_target_pairs={{0,12},{4,0},{8,4},{12,8},{1,13},{5,1},{9,5},{13,9},{2,14},{6,2},{... | collective-permute-start | bytes 1400840 | tf_op jit(solution)/shard_map/tokens/ppermute | solution.py:236
  38.6 74.1 %all-to-all-start = ((bf16[128,8,1152]{2,1,0:T(8,128)(2,1)}), bf16[128,8,1152]{2,1,0:T(8,128)(2,1)S(1)}, u32[]{:S(2)}, u32[]{:S(2)}) async-start(bf16[128,8,1152]{2,1,0:T(8,128)(2,1)} %bitcast.5.buffer_ref), calls=%async_computation | async-start | bytes 4718592 | tf_op jit(solution)/shard_map/pages/all_to_all | solution.py:326
  51.1 17.1 %collective-permute-start = (bf16[64,7296]{1,0:T(8,128)(2,1)S(1)}, bf16[64,7296]{1,0:T(8,128)(2,1)S(1)}, u32[]{:S(2)}, u32[]{:S(2)}) collective-permute-start(bf16[64,7296]{1,0:T(8,128)(2,1)S(1)} %pad_maximum_fusion.9), channel_id=1, source_target_pairs={{0,128},{128,0},{1,129},{129,1},{2,130},{130,2},{3,131},{131,3},{4... | collective-permute-start | bytes 2801672 | tf_op jit(solution)/shard_map/experts/while/body/ppermute | solution.py:22
  52.2 14.7 %collective-permute-start.1 = (bf16[16,7296]{1,0:T(8,128)(2,1)S(1)}, bf16[16,7296]{1,0:T(8,128)(2,1)S(1)}, u32[]{:S(2)}, u32[]{:S(2)}) collective-permute-start(bf16[16,7296]{1,0:T(8,128)(2,1)S(1)} %slice.263), channel_id=1, source_target_pairs={{0,4},{4,8},{8,12},{12,0},{1,5},{5,9},{9,13},{13,1},{2,6},{6,10},{... | collective-permute-start | bytes 700424 | tf_op jit(solution)/shard_map/experts/while/body/ppermute | solution.py:236
  52.7 14.2 %collective-permute-start.2 = (bf16[16,7296]{1,0:T(8,128)(2,1)S(1)}, bf16[16,7296]{1,0:T(8,128)(2,1)S(1)}, u32[]{:S(2)}, u32[]{:S(2)}) collective-permute-start(bf16[16,7296]{1,0:T(8,128)(2,1)S(1)} %slice.264), channel_id=1, source_target_pairs={{0,12},{4,0},{8,4},{12,8},{1,13},{5,1},{9,5},{13,9},{2,14},{6,2},{... | collective-permute-start | bytes 700424 | tf_op jit(solution)/shard_map/experts/while/body/ppermute | solution.py:236
  68.0 2.6 %collective-permute-start.3 = (bf16[64,7296]{1,0:T(8,128)(2,1)S(1)}, bf16[64,7296]{1,0:T(8,128)(2,1)S(1)}, u32[]{:S(2)}, u32[]{:S(2)}) collective-permute-start(bf16[64,7296]{1,0:T(8,128)(2,1)S(1)} %pad_maximum_fusion.10), channel_id=1, source_target_pairs={{0,128},{128,0},{1,129},{129,1},{2,130},{130,2},{3,131},{131,3},{4... | collective-permute-start | bytes 2801672 | tf_op jit(solution)/shard_map/experts/while/body/ppermute | solution.py:22
  68.2 2.6 %copy-start.6 = (bf16[1,7168,256]{2,1,0:T(8,128)(2,1)S(1)}, bf16[1,7168,256]{2,1,0:T(8,128)(2,1)}, u32[]{:S(2)}) copy-start(bf16[1,7168,256]{2,1,0:T(8,128)(2,1)} %get-tuple-element.357) | copy-start | bytes 11010052 | tf_op jit(solution)/shard_map/experts/while
  70.9 1.5 %copy-start.5 = (bf16[1,128,7168]{2,1,0:T(8,128)(2,1)S(1)}, bf16[1,128,7168]{2,1,0:T(8,128)(2,1)}, u32[]{:S(2)}) copy-start(bf16[1,128,7168]{2,1,0:T(8,128)(2,1)} %get-tuple-element.358) | copy-start | bytes 5505028 | tf_op jit(solution)/shard_map/experts/while
  72.8 2.6 %collective-permute-start.4 = (bf16[64,7168]{1,0:T(8,128)(2,1)S(1)}, bf16[64,7168]{1,0:T(8,128)(2,1)S(1)}, u32[]{:S(2)}, u32[]{:S(2)}) collective-permute-start(bf16[64,7168]{1,0:T(8,128)(2,1)S(1)} %fusion.64), channel_id=1, source_target_pairs={{0,128},{128,0},{1,129},{129,1},{2,130},{130,2},{3,131},{131,3},{4... | collective-permute-start | bytes 2752520 | tf_op jit(solution)/shard_map/experts/while/body/ppermute | solution.py:22
  74.2 6.3 %collective-permute-start.5 = (bf16[64,7168]{1,0:T(8,128)(2,1)S(1)}, bf16[64,7168]{1,0:T(8,128)(2,1)S(1)}, u32[]{:S(2)}, u32[]{:S(2)}) collective-permute-start(bf16[64,7168]{1,0:T(8,128)(2,1)S(1)} %fusion.69), channel_id=1, source_target_pairs={{0,128},{128,0},{1,129},{129,1},{2,130},{130,2},{3,131},{131,3},{4... | collective-permute-start | bytes 2752520 | tf_op jit(solution)/shard_map/experts/while/body/ppermute | solution.py:22
  77.1 13.8 %collective-permute-start.6 = (bf16[16,7168]{1,0:T(8,128)(2,1)S(1)}, bf16[16,7168]{1,0:T(8,128)(2,1)S(1)}, u32[]{:S(2)}, u32[]{:S(2)}) collective-permute-start(bf16[16,7168]{1,0:T(8,128)(2,1)S(1)} %get-tuple-element.326), channel_id=1, source_target_pairs={{0,12},{4,0},{8,4},{12,8},{1,13},{5,1},{9,5},{13,9},{2,14},{6,2},{... | collective-permute-start | bytes 688136 | tf_op jit(solution)/shard_map/experts/while/body/ppermute | solution.py:236
  77.2 13.8 %collective-permute-start.7 = (bf16[16,7168]{1,0:T(8,128)(2,1)S(1)}, bf16[16,7168]{1,0:T(8,128)(2,1)S(1)}, u32[]{:S(2)}, u32[]{:S(2)}) collective-permute-start(bf16[16,7168]{1,0:T(8,128)(2,1)S(1)} %get-tuple-element.327), channel_id=1, source_target_pairs={{0,4},{4,8},{8,12},{12,0},{1,5},{5,9},{9,13},{13,1},{2,6},{6,10},{... | collective-permute-start | bytes 688136 | tf_op jit(solution)/shard_map/experts/while/body/ppermute | solution.py:236
  91.9 14.4 %collective-permute-start.8 = (bf16[32,7168]{1,0:T(8,128)(2,1)}, bf16[32,7168]{1,0:T(8,128)(2,1)}, u32[]{:S(2)}, u32[]{:S(2)}) collective-permute-start(bf16[32,7168]{1,0:T(8,128)(2,1)} %pad_maximum_fusion.11), channel_id=1, source_target_pairs={{0,4},{4,8},{8,12},{12,0},{1,5},{5,9},{9,13},{13,1},{2,6},{6,10},{... | collective-permute-start | bytes 1376264 | tf_op jit(solution)/shard_map/experts/while/body/ppermute | solution.py:236
  94.3 15.5 %collective-permute-start.9 = (bf16[32,7168]{1,0:T(8,128)(2,1)}, bf16[32,7168]{1,0:T(8,128)(2,1)}, u32[]{:S(2)}, u32[]{:S(2)}) collective-permute-start(bf16[32,7168]{1,0:T(8,128)(2,1)} %pad_maximum_fusion.12), channel_id=1, source_target_pairs={{0,12},{4,0},{8,4},{12,8},{1,13},{5,1},{9,5},{13,9},{2,14},{6,2},{... | collective-permute-start | bytes 1376264 | tf_op jit(solution)/shard_map/experts/while/body/ppermute | solution.py:236
  112.7 1.4 %copy-start = (bf16[128,8,1152]{2,1,0:T(8,128)(2,1)}, bf16[128,8,1152]{2,1,0:T(8,128)(2,1)S(1)}, u32[]{:S(2)}) copy-start(bf16[128,8,1152]{2,1,0:T(8,128)(2,1)S(1)} %all-to-all-done.pages_ref.beside_ref) | copy-start | bytes 7077892
  116.0 7.9 %copy-start.3 = (f32[256,512]{1,0:T(8,128)S(1)}, f32[256,512]{1,0:T(8,128)}, u32[]{:S(2)}) copy-start(f32[256,512]{1,0:T(8,128)} %copy-done.2) | copy-start | bytes 1572868
  116.0 23.4 %all-to-all-start.2 = ((bf16[32,8,896]{2,1,0:T(8,128)(2,1)}), bf16[32,8,896]{2,1,0:T(8,128)(2,1)S(1)}, u32[]{:S(2)}, u32[]{:S(2)}) async-start(bf16[32,8,896]{2,1,0:T(8,128)(2,1)} %pass.1), calls=%async_computation.2 | async-start | bytes 917504 | tf_op jit(solution)/shard_map/sums/all_to_all | solution.py:354
  123.9 1.7 %copy-start.1 = (bf16[128,8,1152]{2,1,0:T(8,128)(2,1)S(1)}, bf16[128,8,1152]{2,1,0:T(8,128)(2,1)}, u32[]{:S(2)}) copy-start(bf16[128,8,1152]{2,1,0:T(8,128)(2,1)} %copy-done) | copy-start | bytes 7077892

commit v2 on v1

--- a/solution.py
+++ b/solution.py
@@ -16,6 +16,7 @@
 EMPTY = 128.0
 LANES = 128
 FOLD = 8
+SMALL = pltpu.CompilerParams(vmem_limit_bytes=6 * 1024 * 1024)
 
 
 def swap(value):
@@ -82,7 +83,7 @@
             pl.BlockSpec((rows, LANES), lambda i: (0, 0)),
         ],
         out_shape=[jax.ShapeDtypeStruct((rows, WIDTH), jnp.float32), stat, stat],
-        compiler_params=pltpu.CompilerParams(vmem_limit_bytes=32 * 1024 * 1024),
+        compiler_params=pltpu.CompilerParams(vmem_limit_bytes=20 * 1024 * 1024),
         cost_estimate=pl.CostEstimate(
             flops=2 * rows * keys * (latent + WIDTH), bytes_accessed=4 * 1024 * 1024, transcendentals=rows * keys
         ),
@@ -154,7 +155,7 @@
             pltpu.VMEM((rows, LANES), jnp.float32),
             pltpu.VMEM((rows, LANES), jnp.float32),
         ],
-        compiler_params=pltpu.CompilerParams(vmem_limit_bytes=32 * 1024 * 1024),
+        compiler_params=pltpu.CompilerParams(vmem_limit_bytes=20 * 1024 * 1024),
         cost_estimate=pl.CostEstimate(
             flops=2 * rows * keys * (2 * WIDTH + LANES), bytes_accessed=4 * 1024 * 1024, transcendentals=rows * keys
         ),
@@ -194,7 +195,7 @@
     return pl.pallas_call(
         slots_kernel,
         out_shape=jax.ShapeDtypeStruct((peers * page, wide), jnp.bfloat16),
-        compiler_params=pltpu.CompilerParams(vmem_limit_bytes=32 * 1024 * 1024),
+        compiler_params=pltpu.CompilerParams(vmem_limit_bytes=20 * 1024 * 1024),
         cost_estimate=pl.CostEstimate(flops=2 * (peers * page) ** 2 * wide, bytes_accessed=4 * 1024 * 1024, transcendentals=0),
         name="slots",
     )(owners, pages).reshape(peers, page, wide)
@@ -222,11 +223,11 @@
     out_ref[:, rows * part :] = scratch_ref[:, 0, part:].astype(jnp.bfloat16)
 
 
-def fold_kernel(far_ref, after_ref, before_ref, out_ref, scratch_ref):
+def fold_kernel(own_ref, after_ref, before_ref, out_ref, scratch_ref):
     rows, fold, part = out_ref.shape
     for k in range(fold):
         columns = slice(k * part, (k + 1) * part)
-        term = far_ref[:rows, columns] + after_ref[:, columns].astype(jnp.float32) + before_ref[:, columns].astype(jnp.float32)
+        term = own_ref[:, columns] + after_ref[:, columns].astype(jnp.float32) + before_ref[:, columns].astype(jnp.float32)
         scratch_ref[:, k, :] = term
     out_ref[...] = scratch_ref[...].astype(jnp.bfloat16)
 
@@ -249,56 +250,45 @@
         in_specs=[pl.BlockSpec(memory_space=pltpu.VMEM)] + [pl.BlockSpec(memory_space=pl.ANY)] * 2,
         out_shape=jax.ShapeDtypeStruct((slab, model + LANES), jnp.bfloat16),
         scratch_shapes=[pltpu.VMEM((slab, FOLD, wide), jnp.float32)],
+        compiler_params=SMALL,
         name="unfold",
     )(got, *beside)
 
 
-def expert_part(tokens, w_in, w_out, my_expert):
+def expert_term(tokens, w_in, w_out, my_expert):
     model = w_in.shape[0]
-    own = tokens.shape[0]
-    tokens = jnp.concatenate([tokens, swap(tokens)], axis=0)
     experts = lax.broadcasted_iota(jnp.int32, (1, LANES), 1)
     row_weight = jnp.sum(jnp.where(experts == my_expert, tokens[:, model:].astype(jnp.float32), 0.0), axis=1)
     both = dot(tokens[:, :model], w_in)
     units = both.shape[1] // 2
     hidden = (jax.nn.silu(both[:, :units]) * both[:, units:]).astype(jnp.bfloat16)
-    sent = (dot(hidden[own:], w_out) * row_weight[own:, None]).astype(jnp.bfloat16)
-    got = swap(sent)
-    return dot(hidden[:own], w_out) * row_weight[:own, None] + got.astype(jnp.float32)
+    return dot(hidden, w_out) * row_weight[:, None]
+
+
+def expert_part(tokens, *rest):
+    sent = expert_term(swap(tokens), *rest).astype(jnp.bfloat16)
+    return expert_term(tokens, *rest) + swap(sent).astype(jnp.float32)
 
 
 def experts_sum(slab, before, after, w_in, w_out, my_expert):
     rows = slab.shape[0]
     half = rows // 2
     first, second = shift(before[:half], 1), shift(after[half:], -1)
-    near = expert_part(jnp.concatenate([before, after], axis=0), w_in, w_out, my_expert)
-    far = expert_part(jnp.concatenate([slab, first, second], axis=0), w_in, w_out, my_expert)
-    opposite = far[rows:].astype(jnp.bfloat16)
+    near = expert_part(jnp.concatenate([before, after, slab], axis=0), w_in, w_out, my_expert)
+    far = expert_part(jnp.concatenate([first, second], axis=0), w_in, w_out, my_expert)
+    opposite = far.astype(jnp.bfloat16)
     top, bottom = shift(opposite[:half], 1), shift(opposite[half:], -1)
     near_before = jnp.concatenate([near[:half], near[half:rows] + bottom.astype(jnp.float32)], axis=0)
-    near_after = jnp.concatenate([near[rows : rows + half] + top.astype(jnp.float32), near[rows + half :]], axis=0)
-    terms = (far, shift(near_after.astype(jnp.bfloat16), 1), shift(near_before.astype(jnp.bfloat16), -1))
+    near_after = jnp.concatenate([near[rows : rows + half] + top.astype(jnp.float32), near[rows + half : 2 * rows]], axis=0)
+    terms = (near[2 * rows :], shift(near_after.astype(jnp.bfloat16), 1), shift(near_before.astype(jnp.bfloat16), -1))
     folded = (rows, FOLD, far.shape[1] // FOLD)
     return pl.pallas_call(
         fold_kernel,
         out_shape=jax.ShapeDtypeStruct(folded, jnp.bfloat16),
         scratch_shapes=[pltpu.VMEM(folded, jnp.float32)],
+        compiler_params=SMALL,
         name="fold",
     )(*terms)
-
-
-def pass_kernel(value_ref, beside_ref, out_ref):
-    out_ref[...] = value_ref[...]
-
-
-def after_both(value, beside):
-    vmem = pl.BlockSpec(memory_space=pltpu.VMEM)
-    return pl.pallas_call(
-        pass_kernel,
-        in_specs=[vmem, pl.BlockSpec(memory_space=pl.ANY)],
-        out_shape=jax.ShapeDtypeStruct(value.shape, value.dtype),
-        name="pass",
-    )(value, beside)
 
 
 def local(
@@ -351,7 +341,8 @@
         sums = lax.fori_loop(0, lax.optimization_barrier(jnp.int32(1)), turn, blank)
 
     with jax.named_scope("sums"):
-        ends = lax.all_to_all(after_both(sums, arrived), SLAB, 0, 0, tiled=True)
+        sums, arrived = lax.optimization_barrier((sums, arrived))
+        ends = lax.all_to_all(sums, SLAB, 0, 0, tiled=True)
         mixed = jnp.sum(ends.astype(jnp.float32), axis=0).reshape(1, model).astype(jnp.bfloat16)
 
     with jax.named_scope("attention"):

time: 141 us -> 133 us (0.943)
  Pallas kernels: 24.4 us -> 19.8 us
  waiting for transfers between devices: 52.6 us -> 49.6 us
    unnamed x16 -> x12, local copies, waits for them, and re-layouts: 8.15 us -> 3.47 us
    ppermute x6, waiting for transfers between devices: 2.93 us -> 0.41 us  [swap(): return lax.ppermute(value, 'pool', [(0, 1), (1, 0)])]
    concatenate x2 -> x0, other arithmetic: 2.17 us -> none  [the longest x1 1.09 us: experts_sum(): jnp.concatenate([slab, first, second], axis=0)]
    pallas_call x1 -> x0, Pallas kernels: 1.84 us -> none  [after_both(): pl.pallas_call(pass_kernel, in_specs=[vmem, pl.BlockSpec(memory_space=pl....]
    pallas_call x1, Pallas kernels: 2.95 us -> 1.25 us  [experts_sum(): pl.pallas_call(fold_kernel, out_shape=jax.ShapeDtypeStruct(folded, jnp.bf...]
    dot_general x6 -> x8, matrix products: 4.39 us -> 4.88 us  [dot(): return jnp.dot(a, b, preferred_element_type=jnp.float32)]
    while x8 -> x9, local copies, waits for them, and re-layouts: 3.01 us -> 2.79 us
  transfers between devices with their start and end apart: 17 -> 17, of which waited for: 9 -> 11; matrix products, arithmetic and copies ran while one was open for 10% -> 13% of each run, Pallas kernels for 13% -> 13%
where the time goes in v2:
time: 133 us; the launch traced here: 132 us
  waiting for transfers between devices  49.6 us (37%)
  starting transfers between devices  40.3 us (30%)
  Pallas kernels  19.8 us (15%)
  local copies, waits for them, and re-layouts  13.3 us (10%)
  matrix products  4.88 us (4%)
  other arithmetic  3.03 us (2%)
  between operations  1.43 us (1%)
    ppermute x8, waiting for transfers between devices, shift(): lax.ppermute(value, 'y', [(i, (i + by) % count) for i in range(count)])  35 us
    all_to_all x1, starting transfers between devices, gather_slab(): got = lax.all_to_all(sent, SLAB, 0, 0, tiled=True)  11.3 us
    all_to_all x1, waiting for transfers between devices, local(): ends = lax.all_to_all(sums, SLAB, 0, 0, tiled=True)  9.55 us
    ppermute x8, starting transfers between devices, shift(): lax.ppermute(value, 'y', [(i, (i + by) % count) for i in range(count)])  9.54 us
    all_to_all x1, starting transfers between devices, local(): ends = lax.all_to_all(sums, SLAB, 0, 0, tiled=True)  9.1 us
    all_to_all x1, starting transfers between devices, local(): arrived = lax.all_to_all(buffer, CHIPS, 0, 0, tiled=True)  8.82 us
    pallas_call x1, Pallas kernels, slot_buffer(): pl.pallas_call(slots_kernel, out_shape=jax.ShapeDtypeStruct((peers * page...  5.75 us
    dot_general x8, matrix products, dot(): return jnp.dot(a, b, preferred_element_type=jnp.float32)  4.88 us
  transfers between devices with their start and end apart: 17, of which 11 were waited for; matrix products, arithmetic and copies ran while one was open for 13% of the time, Pallas kernels for 13%

profile of v2, /device:TPU:24, one launch (start us, length us, event | category | flops | bytes accessed | tf_op | source)
XLA Modules:
  0.0 132.4 jit_solution(3282986741800678832)
XLA Ops:
  0.6 0.1 collective-permute-start.11
  0.7 1.7 %token_.1 = bf16[32,8,1024]{2,1,0:T(8,128)(2,1)} custom-call(bf16[1,7168]{1,0:T(2,128)(2,1)} %input_ref.1, s32[1,8]{1,0:T(1,128)} %ids_ref.1, bf16[1,8]{1,0:T(2,128)(2,1)} %gates_ref.1), custom_call_target="tpu_custom_call" | custom-call | tf_op jit(solution)/shard_map/tokens/token/pallas_call | solution.py:244
  2.4 11.3 %all-to-all-start = ((bf16[32,8,1024]{2,1,0:T(8,128)(2,1)}), bf16[32,8,1024]{2,1,0:T(8,128)(2,1)S(1)}, u32[]{:S(2)}, u32[]{:S(2)}) async-start(bf16[32,8,1024]{2,1,0:T(8,128)(2,1)} %token_.1), calls=%async_computation | async-start | bytes 1048576 | tf_op jit(solution)/shard_map/tokens/all_to_all | solution.py:247
  13.8 0.3 collective-permute-start.10
  14.1 1.2 copy.13
  15.9 1.7 %copy-done.3 = bf16[1,2048,576]{1,2,0:T(8,128)(2,1)S(1)} copy-done((bf16[1,2048,576]{1,2,0:T(8,128)(2,1)S(1)}, bf16[1,2048,576]{1,2,0:T(8,128)(2,1)}, u32[]{:S(2)}) %copy-start.3) | copy-done | bytes 2359320
  17.6 4.2 %resident.1 = (f32[256,512]{1,0:T(8,128)S(1)}, f32[256,128]{1,0:T(8,128)S(1)}, f32[256,128]{1,0:T(8,128)S(1)}) custom-call(s32[1]{0:T(128)S(6)} %copy.26.length_ref, bf16[256,576]{1,0:T(8,128)(2,1)S(1)} %bitcast.58, bf16[16,576]{1,0:T(8,128)(2,1)S(1)} %concatenate.41.own_ref, bf16[576,2048]{1,0:T(8,128)(2,1)S(1)} %bitcast.61), custom_call_target="tpu_custom_call" | custom-call | flops 1140850688 | bytes 4194304 | tf_op jit(solution)/shard_map/resident/resident/pallas_call | solution.py:71
  21.8 5.8 %slots.1 = bf16[1024,1152]{1,0:T(8,128)(2,1)} custom-call(s32[1,128]{1,0:T(1,128)S(1)} %collective-permute-done.10.owner_ref, bf16[8,576,128]{2,1,0:T(8,128)(2,1)S(1)} %collective-permute-done.11.pages_ref), custom_call_target="tpu_custom_call" | custom-call | flops 2415919104 | bytes 4194304 | tf_op jit(solution)/shard_map/pages/slots/pallas_call | solution.py:195
  27.6 4.6 %all-to-all-done.folded_ref = bf16[32,8,1024]{2,1,0:T(8,128)(2,1)S(1)} async-done(((bf16[32,8,1024]{2,1,0:T(8,128)(2,1)}), bf16[32,8,1024]{2,1,0:T(8,128)(2,1)S(1)}, u32[]{:S(2)}, u32[]{:S(2)}) %all-to-all-start) | async-done | bytes 524320 | tf_op jit(solution)/shard_map/tokens/all_to_all | solution.py:247
  32.1 2.6 %unfold.1 = bf16[32,7296]{1,0:T(8,128)(2,1)} custom-call(bf16[32,8,1024]{2,1,0:T(8,128)(2,1)S(1)} %all-to-all-done.folded_ref, bf16[128,8,1152]{2,1,0:T(8,128)(2,1)} %bitcast.5.buffer_ref, f32[256,512]{1,0:T(8,128)S(1)} %get-tuple-element.193.partial_ref.acc_in_ref), custom_call_target="tpu_custom_call" | custom-call | tf_op jit(solution)/shard_map/tokens/unfold/pallas_call | solution.py:248
  34.7 0.2 collective-permute-start.12
  34.9 1.8 %collective-permute-start.13 = (bf16[32,7296]{1,0:T(8,128)(2,1)}, bf16[32,7296]{1,0:T(8,128)(2,1)}, u32[]{:S(2)}, u32[]{:S(2)}) collective-permute-start(bf16[32,7296]{1,0:T(8,128)(2,1)} %unfold.1), channel_id=1, source_target_pairs={{0,12},{4,0},{8,4},{12,8},{1,13},{5,1},{9,5},{13,9},{2,14},{6,2},{... | collective-permute-start | bytes 1400840 | tf_op jit(solution)/shard_map/tokens/ppermute | solution.py:237
  36.7 8.8 %all-to-all-start.1 = ((bf16[128,8,1152]{2,1,0:T(8,128)(2,1)}), bf16[128,8,1152]{2,1,0:T(8,128)(2,1)S(1)}, u32[]{:S(2)}, u32[]{:S(2)}) async-start(bf16[128,8,1152]{2,1,0:T(8,128)(2,1)} %bitcast.5.buffer_ref), calls=%async_computation.1 | async-start | bytes 4718592 | tf_op jit(solution)/shard_map/pages/all_to_all | solution.py:316
  45.6 0.8 collective-permute-done.12
  46.4 2.3 %collective-permute-done.13 = bf16[32,7296]{1,0:T(8,128)(2,1)} collective-permute-done((bf16[32,7296]{1,0:T(8,128)(2,1)}, bf16[32,7296]{1,0:T(8,128)(2,1)}, u32[]{:S(2)}, u32[]{:S(2)}) %collective-permute-start.13) | collective-permute-done | bytes 466976 | tf_op jit(solution)/shard_map/tokens/ppermute | solution.py:237
  48.7 0.8 broadcast_in_dim.54
  49.5 56.2 %while.13 = (s32[]{:T(128)}, bf16[32,8,896]{2,1,0:T(8,128)(2,1)}, s32[]{:T(128)}, bf16[32,7296]{1,0:T(8,128)(2,1)}, bf16[32,7296]{1,0:T(8,128)(2,1)}, /*index=5*...) while((s32[]{:T(128)}, bf16[32,8,896]{2,1,0:T(8,128)(2,1)}, ...), condition=%wide.region_5.6_spmd, body=%wide.region_0.5_spmd.sunk | while | flops 1417609088 | bytes 101764040 | solution.py:341
  49.5 1.0 slice.282
  50.4 0.1 collective-permute-start.2
  50.5 1.0 slice.283
  51.5 0.0 copy-start.4
  51.5 2.1 %collective-permute-start.3 = (bf16[16,7296]{1,0:T(8,128)(2,1)S(1)}, bf16[16,7296]{1,0:T(8,128)(2,1)S(1)}, u32[]{:S(2)}, u32[]{:S(2)}) collective-permute-start(bf16[16,7296]{1,0:T(8,128)(2,1)S(1)} %slice.283), channel_id=1, source_target_pairs={{0,12},{4,0},{8,4},{12,8},{1,13},{5,1},{9,5},{13,9},{2,14},{6,2},{... | collective-permute-start | bytes 700424 | tf_op jit(solution)/shard_map/experts/while/body/ppermute | solution.py:237
  53.6 1.1 constant_dynamic-update-slice_fusion.10
  54.6 1.1 constant_dynamic-update-slice_fusion.11
  55.7 6.0 %collective-permute-done.2 = bf16[16,7296]{1,0:T(8,128)(2,1)S(1)} collective-permute-done((bf16[16,7296]{1,0:T(8,128)(2,1)S(1)}, bf16[16,7296]{1,0:T(8,128)(2,1)S(1)}, u32[]{:S(2)}, u32[]{:S(2)}) %collective-permute-start.2) | collective-permute-done | bytes 233504 | tf_op jit(solution)/shard_map/experts/while/body/ppermute | solution.py:237
  61.7 0.1 collective-permute-start.4
  61.8 1.1 constant_dynamic-update-slice_fusion.12
  62.9 0.6 collective-permute-start
  63.5 0.2 collective-permute-done.4
  63.7 0.7 fusion.93
  64.4 0.1 select_reduce_fusion.7
  64.5 0.6 copy-done.5
  65.2 0.4 multiply_convert_fusion.5
  65.5 0.2 collective-permute-start.5
  65.8 0.7 fusion.90
  66.5 0.7 fusion.94
  67.2 0.2 collective-permute-done.5
  67.4 0.4 add_convert_fusion.2
  67.8 0.1 select_reduce_fusion.6
  68.0 0.8 fusion.89
  68.7 0.5 multiply_convert_fusion.4
  69.3 0.2 collective-permute-start.1
  69.5 0.6 collective-permute-start.6
  70.2 2.7 %collective-permute-start.7 = (bf16[16,7168]{1,0:T(8,128)(2,1)S(1)}, bf16[16,7168]{1,0:T(8,128)(2,1)S(1)}, u32[]{:S(2)}, u32[]{:S(2)}) collective-permute-start(bf16[16,7168]{1,0:T(8,128)(2,1)S(1)} %get-tuple-element.313), channel_id=1, source_target_pairs={{0,4},{4,8},{8,12},{12,0},{1,5},{5,9},{9,13},{13,1},{2,6},{6,10},{... | collective-permute-start | bytes 688136 | tf_op jit(solution)/shard_map/experts/while/body/ppermute | solution.py:237
  72.9 0.7 fusion.91
  73.6 8.5 %collective-permute-done.6 = bf16[16,7168]{1,0:T(8,128)(2,1)S(1)} collective-permute-done((bf16[16,7168]{1,0:T(8,128)(2,1)S(1)}, bf16[16,7168]{1,0:T(8,128)(2,1)S(1)}, u32[]{:S(2)}, u32[]{:S(2)}) %collective-permute-start.6) | collective-permute-done | bytes 229408 | tf_op jit(solution)/shard_map/experts/while/body/ppermute | solution.py:237
  82.1 0.8 collective-permute-done.7
  82.9 0.1 fusion.96
  83.0 0.8 pad_maximum_fusion.5
  83.8 1.1 collective-permute-start.8
  84.8 0.8 pad_maximum_fusion.6
  85.6 1.0 collective-permute-start.9
  86.6 1.2 slice.281.own_ref
  87.8 12.6 %collective-permute-done.8.after_ref = bf16[32,7168]{1,0:T(8,128)(2,1)S(1)} collective-permute-done((bf16[32,7168]{1,0:T(8,128)(2,1)}, bf16[32,7168]{1,0:T(8,128)(2,1)S(1)}, u32[]{:S(2)}, u32[]{:S(2)}) %collective-permute-start.8) | collective-permute-done | bytes 458784 | tf_op jit(solution)/shard_map/experts/while/body/ppermute | solution.py:237
  100.4 4.1 %collective-permute-done.9.before_ref = bf16[32,7168]{1,0:T(8,128)(2,1)S(1)} collective-permute-done((bf16[32,7168]{1,0:T(8,128)(2,1)}, bf16[32,7168]{1,0:T(8,128)(2,1)S(1)}, u32[]{:S(2)}, u32[]{:S(2)}) %collective-permute-start.9) | collective-permute-done | bytes 458784 | tf_op jit(solution)/shard_map/experts/while/body/ppermute | solution.py:237
  104.5 1.3 fold.4
  105.7 9.1 %all-to-all-start.2 = ((bf16[32,8,896]{2,1,0:T(8,128)(2,1)}), bf16[32,8,896]{2,1,0:T(8,128)(2,1)}, u32[]{:S(2)}, u32[]{:S(2)}) async-start(bf16[32,8,896]{2,1,0:T(8,128)(2,1)} %get-tuple-element.198), calls=%async_computation.2 | async-start | bytes 917504 | tf_op jit(solution)/shard_map/sums/all_to_all | solution.py:345
  114.8 1.0 slice.180
  115.8 0.8 slice.181
  116.7 0.1 fusion.52
  116.8 4.4 %arrived.1 = bf16[256,512]{1,0:T(8,128)(2,1)} custom-call(bf16[272,512]{1,0:T(8,128)(2,1)S(1)} %pad_maximum_fusion.2.wide_ref, bf16[256,128]{1,0:T(8,128)(2,1)S(1)} %get-tuple-element.232.low_ref, bf16[256,128]{1,0:T(8,128)(2,1)S(1)} %get-tuple-element.231.high_ref, bf16[128,8,1152]{2,1,0:T(8,128)(2,1)S(1)} %all-to-all-done.1.pages_ref, ...), custom_call_target="tpu_custom_call" | custom-call | flops 1207959552 | bytes 4194304 | tf_op jit(solution)/shard_map/attention/arrived/pallas_call | solution.py:147
  121.2 9.6 %all-to-all-done.2 = bf16[32,8,896]{2,1,0:T(8,128)(2,1)} async-done(((bf16[32,8,896]{2,1,0:T(8,128)(2,1)}), bf16[32,8,896]{2,1,0:T(8,128)(2,1)}, u32[]{:S(2)}, u32[]{:S(2)}) %all-to-all-start.2) | async-done | bytes 458784 | tf_op jit(solution)/shard_map/sums/all_to_all | solution.py:345
  130.7 1.1 reduce_sum.60
  131.8 0.6 copy.15
  (28 shorter events, 0.2 us)
Async XLA Ops:
  0.6 15.2 %copy-start.7 = (bf16[2,1,576]{2,0,1:T(2,128)(2,1)S(1)}, bf16[2,1,576]{2,0,1:T(2,128)(2,1)}, u32[]{:S(2)}) copy-start(bf16[2,1,576]{2,0,1:T(2,128)(2,1)} %param.14) | copy-start | bytes 6916
  0.6 21.2 %collective-permute-start.11 = (bf16[8,576,128]{2,1,0:T(8,128)(2,1)}, bf16[8,576,128]{2,1,0:T(8,128)(2,1)S(1)}, u32[]{:S(2)}, u32[]{:S(2)}) collective-permute-start(bf16[8,576,128]{2,1,0:T(8,128)(2,1)} %bitcast.65), channel_id=1, source_target_pairs={{0,128},{128,0},{1,129},{129,1},{2,130},{130,2},{3,131},{131,3},{4... | collective-permute-start | bytes 3538952 | tf_op jit(solution)/shard_map/pages/ppermute | solution.py:23
  2.4 29.7 %all-to-all-start = ((bf16[32,8,1024]{2,1,0:T(8,128)(2,1)}), bf16[32,8,1024]{2,1,0:T(8,128)(2,1)S(1)}, u32[]{:S(2)}, u32[]{:S(2)}) async-start(bf16[32,8,1024]{2,1,0:T(8,128)(2,1)} %token_.1), calls=%async_computation | async-start | bytes 1048576 | tf_op jit(solution)/shard_map/tokens/all_to_all | solution.py:247
  13.8 8.0 %collective-permute-start.10 = (s32[1,128]{1,0:T(1,128)}, s32[1,128]{1,0:T(1,128)S(1)}, u32[]{:S(2)}, u32[]{:S(2)}) collective-permute-start(s32[1,128]{1,0:T(1,128)} %bitcast.66), channel_id=1, source_target_pairs={{0,128},{128,0},{1,129},{129,1},{2,130},{130,2},{3,131},{131,3},{4... | collective-permute-start | bytes 1544 | tf_op jit(solution)/shard_map/pages/ppermute | solution.py:23
  15.2 6.5 %copy-start = (bf16[2,1,128,576]{3,2,0,1:T(8,128)(2,1)}, bf16[2,1,128,576]{3,2,0,1:T(8,128)(2,1)S(1)}, u32[]{:S(2)}) copy-start(bf16[2,1,128,576]{3,2,0,1:T(8,128)(2,1)S(1)} %copy.13) | copy-start | bytes 884740
  15.9 1.7 %copy-start.3 = (bf16[1,2048,576]{1,2,0:T(8,128)(2,1)S(1)}, bf16[1,2048,576]{1,2,0:T(8,128)(2,1)}, u32[]{:S(2)}) copy-start(bf16[1,2048,576]{1,2,0:T(8,128)(2,1)} %param.15) | copy-start | bytes 7077892
  21.8 10.4 %copy-start.1 = (f32[256,512]{1,0:T(8,128)}, f32[256,512]{1,0:T(8,128)S(1)}, u32[]{:S(2)}) copy-start(f32[256,512]{1,0:T(8,128)S(1)} %get-tuple-element.193.partial_ref.acc_in_ref) | copy-start | bytes 1572868
  34.7 11.7 %collective-permute-start.12 = (bf16[32,7296]{1,0:T(8,128)(2,1)}, bf16[32,7296]{1,0:T(8,128)(2,1)}, u32[]{:S(2)}, u32[]{:S(2)}) collective-permute-start(bf16[32,7296]{1,0:T(8,128)(2,1)} %unfold.1), channel_id=1, source_target_pairs={{0,4},{4,8},{8,12},{12,0},{1,5},{5,9},{9,13},{13,1},{2,6},{6,10},{... | collective-permute-start | bytes 1400840 | tf_op jit(solution)/shard_map/tokens/ppermute | solution.py:237
  34.9 13.7 %collective-permute-start.13 = (bf16[32,7296]{1,0:T(8,128)(2,1)}, bf16[32,7296]{1,0:T(8,128)(2,1)}, u32[]{:S(2)}, u32[]{:S(2)}) collective-permute-start(bf16[32,7296]{1,0:T(8,128)(2,1)} %unfold.1), channel_id=1, source_target_pairs={{0,12},{4,0},{8,4},{12,8},{1,13},{5,1},{9,5},{13,9},{2,14},{6,2},{... | collective-permute-start | bytes 1400840 | tf_op jit(solution)/shard_map/tokens/ppermute | solution.py:237
  36.7 69.0 %all-to-all-start.1 = ((bf16[128,8,1152]{2,1,0:T(8,128)(2,1)}), bf16[128,8,1152]{2,1,0:T(8,128)(2,1)S(1)}, u32[]{:S(2)}, u32[]{:S(2)}) async-start(bf16[128,8,1152]{2,1,0:T(8,128)(2,1)} %bitcast.5.buffer_ref), calls=%async_computation.1 | async-start | bytes 4718592 | tf_op jit(solution)/shard_map/pages/all_to_all | solution.py:316
  50.4 11.3 %collective-permute-start.2 = (bf16[16,7296]{1,0:T(8,128)(2,1)S(1)}, bf16[16,7296]{1,0:T(8,128)(2,1)S(1)}, u32[]{:S(2)}, u32[]{:S(2)}) collective-permute-start(bf16[16,7296]{1,0:T(8,128)(2,1)S(1)} %slice.282), channel_id=1, source_target_pairs={{0,4},{4,8},{8,12},{12,0},{1,5},{5,9},{9,13},{13,1},{2,6},{6,10},{... | collective-permute-start | bytes 700424 | tf_op jit(solution)/shard_map/experts/while/body/ppermute | solution.py:237
  51.5 12.2 %copy-start.4 = (bf16[1,7168,256]{2,1,0:T(8,128)(2,1)S(1)}, bf16[1,7168,256]{2,1,0:T(8,128)(2,1)}, u32[]{:S(2)}) copy-start(bf16[1,7168,256]{2,1,0:T(8,128)(2,1)} %get-tuple-element.343) | copy-start | bytes 11010052 | tf_op jit(solution)/shard_map/experts/while
  51.5 10.2 %collective-permute-start.3 = (bf16[16,7296]{1,0:T(8,128)(2,1)S(1)}, bf16[16,7296]{1,0:T(8,128)(2,1)S(1)}, u32[]{:S(2)}, u32[]{:S(2)}) collective-permute-start(bf16[16,7296]{1,0:T(8,128)(2,1)S(1)} %slice.283), channel_id=1, source_target_pairs={{0,12},{4,0},{8,4},{12,8},{1,13},{5,1},{9,5},{13,9},{2,14},{6,2},{... | collective-permute-start | bytes 700424 | tf_op jit(solution)/shard_map/experts/while/body/ppermute | solution.py:237
  61.7 1.9 %collective-permute-start.4 = (bf16[32,7296]{1,0:T(8,128)(2,1)S(1)}, bf16[32,7296]{1,0:T(8,128)(2,1)S(1)}, u32[]{:S(2)}, u32[]{:S(2)}) collective-permute-start(bf16[32,7296]{1,0:T(8,128)(2,1)S(1)} %constant_dynamic-update-slice_fusion.14), channel_id=1, source_target_pairs={{0,128},{128,0},{1,129},{129,1},{2,130},{130,2},{3,131},{131,3},{4... | collective-permute-start | bytes 1400840 | tf_op jit(solution)/shard_map/experts/while/body/ppermute | solution.py:23
  62.9 4.9 %collective-permute-start = (bf16[96,7296]{1,0:T(8,128)(2,1)S(1)}, bf16[96,7296]{1,0:T(8,128)(2,1)S(1)}, u32[]{:S(2)}, u32[]{:S(2)}) collective-permute-start(bf16[96,7296]{1,0:T(8,128)(2,1)S(1)} %constant_dynamic-update-slice_fusion.12), channel_id=1, source_target_pairs={{0,128},{128,0},{1,129},{129,1},{2,130},{130,2},{3,131},{131,3},{4... | collective-permute-start | bytes 4202504 | tf_op jit(solution)/shard_map/experts/while/body/ppermute | solution.py:23
  63.7 1.5 %copy-start.5 = (bf16[1,128,7168]{2,1,0:T(8,128)(2,1)S(1)}, bf16[1,128,7168]{2,1,0:T(8,128)(2,1)}, u32[]{:S(2)}) copy-start(bf16[1,128,7168]{2,1,0:T(8,128)(2,1)} %get-tuple-element.344) | copy-start | bytes 5505028 | tf_op jit(solution)/shard_map/experts/while
  65.5 1.9 %collective-permute-start.5 = (bf16[32,7168]{1,0:T(8,128)(2,1)S(1)}, bf16[32,7168]{1,0:T(8,128)(2,1)S(1)}, u32[]{:S(2)}, u32[]{:S(2)}) collective-permute-start(bf16[32,7168]{1,0:T(8,128)(2,1)S(1)} %multiply_convert_fusion.5), channel_id=1, source_target_pairs={{0,128},{128,0},{1,129},{129,1},{2,130},{130,2},{3,131},{131,3},{4... | collective-permute-start | bytes 1376264 | tf_op jit(solution)/shard_map/experts/while/body/ppermute | solution.py:23
  69.3 3.6 %collective-permute-start.1 = (bf16[96,7168]{1,0:T(8,128)(2,1)S(1)}, bf16[96,7168]{1,0:T(8,128)(2,1)S(1)}, u32[]{:S(2)}, u32[]{:S(2)}) collective-permute-start(bf16[96,7168]{1,0:T(8,128)(2,1)S(1)} %multiply_convert_fusion.4), channel_id=1, source_target_pairs={{0,128},{128,0},{1,129},{129,1},{2,130},{130,2},{3,131},{131,3},{4... | collective-permute-start | bytes 4128776 | tf_op jit(solution)/shard_map/experts/while/body/ppermute | solution.py:23
  69.5 12.6 %collective-permute-start.6 = (bf16[16,7168]{1,0:T(8,128)(2,1)S(1)}, bf16[16,7168]{1,0:T(8,128)(2,1)S(1)}, u32[]{:S(2)}, u32[]{:S(2)}) collective-permute-start(bf16[16,7168]{1,0:T(8,128)(2,1)S(1)} %get-tuple-element.312), channel_id=1, source_target_pairs={{0,12},{4,0},{8,4},{12,8},{1,13},{5,1},{9,5},{13,9},{2,14},{6,2},{... | collective-permute-start | bytes 688136 | tf_op jit(solution)/shard_map/experts/while/body/ppermute | solution.py:237
  70.2 12.7 %collective-permute-start.7 = (bf16[16,7168]{1,0:T(8,128)(2,1)S(1)}, bf16[16,7168]{1,0:T(8,128)(2,1)S(1)}, u32[]{:S(2)}, u32[]{:S(2)}) collective-permute-start(bf16[16,7168]{1,0:T(8,128)(2,1)S(1)} %get-tuple-element.313), channel_id=1, source_target_pairs={{0,4},{4,8},{8,12},{12,0},{1,5},{5,9},{9,13},{13,1},{2,6},{6,10},{... | collective-permute-start | bytes 688136 | tf_op jit(solution)/shard_map/experts/while/body/ppermute | solution.py:237
  73.5 10.2 %copy-start.6 = (f32[96,7168]{1,0:T(8,128)}, f32[96,7168]{1,0:T(8,128)S(1)}, u32[]{:S(2)}) copy-start(f32[96,7168]{1,0:T(8,128)S(1)} %get-tuple-element.307) | copy-start | bytes 8257540 | tf_op jit(solution)/shard_map/experts/while
  83.8 16.6 %collective-permute-start.8 = (bf16[32,7168]{1,0:T(8,128)(2,1)}, bf16[32,7168]{1,0:T(8,128)(2,1)S(1)}, u32[]{:S(2)}, u32[]{:S(2)}) collective-permute-start(bf16[32,7168]{1,0:T(8,128)(2,1)} %pad_maximum_fusion.5), channel_id=1, source_target_pairs={{0,4},{4,8},{8,12},{12,0},{1,5},{5,9},{9,13},{13,1},{2,6},{6,10},{... | collective-permute-start | bytes 1376264 | tf_op jit(solution)/shard_map/experts/while/body/ppermute | solution.py:237
  85.6 18.8 %collective-permute-start.9 = (bf16[32,7168]{1,0:T(8,128)(2,1)}, bf16[32,7168]{1,0:T(8,128)(2,1)S(1)}, u32[]{:S(2)}, u32[]{:S(2)}) collective-permute-start(bf16[32,7168]{1,0:T(8,128)(2,1)} %pad_maximum_fusion.6), channel_id=1, source_target_pairs={{0,12},{4,0},{8,4},{12,8},{1,13},{5,1},{9,5},{13,9},{2,14},{6,2},{... | collective-permute-start | bytes 1376264 | tf_op jit(solution)/shard_map/experts/while/body/ppermute | solution.py:237
  105.7 11.1 %copy-start.2 = (f32[256,512]{1,0:T(8,128)S(1)}, f32[256,512]{1,0:T(8,128)}, u32[]{:S(2)}) copy-start(f32[256,512]{1,0:T(8,128)} %copy-done.1) | copy-start | bytes 1572868
  105.7 25.0 %all-to-all-start.2 = ((bf16[32,8,896]{2,1,0:T(8,128)(2,1)}), bf16[32,8,896]{2,1,0:T(8,128)(2,1)}, u32[]{:S(2)}, u32[]{:S(2)}) async-start(bf16[32,8,896]{2,1,0:T(8,128)(2,1)} %get-tuple-element.198), calls=%async_computation.2 | async-start | bytes 917504 | tf_op jit(solution)/shard_map/sums/all_to_all | solution.py:345

commit v3 on v2

--- a/solution.py
+++ b/solution.py
@@ -11,7 +11,9 @@
 MASKED = -1e30
 WIDTH = 512
 ROPE = 64
-SLAB = ("z", "x")
+SLAB = ("x", "z")
+SPLIT = 4096
+OFFSETS = (0, -1, 1, 2)
 CHIPS = ("z", "y", "x")
 EMPTY = 128.0
 LANES = 128
@@ -31,7 +33,12 @@
     return jnp.dot(a, b, preferred_element_type=jnp.float32)
 
 
-def resident_kernel(length_ref, query_ref, own_ref, cache_ref, acc_ref, top_ref, total_ref):
+def parts_of(ref):
+    return ref.at[:, :WIDTH], ref.at[:, WIDTH : WIDTH + LANES], ref.at[:, WIDTH + LANES :]
+
+
+def resident_kernel(length_ref, query_ref, own_ref, cache_ref, state_ref):
+    acc_ref, top_ref, total_ref = parts_of(state_ref)
     step = pl.program_id(0)
     rows = cache_ref.shape[1]
     query = query_ref[...]
@@ -67,7 +74,6 @@
     rows, latent = query.shape
     keys = cache.shape[1]
     block = 512
-    stat = jax.ShapeDtypeStruct((rows, LANES), jnp.float32)
     return pl.pallas_call(
         resident_kernel,
         grid=(keys // block,),
@@ -77,12 +83,8 @@
             pl.BlockSpec(own.shape, lambda i: (0, 0)),
             pl.BlockSpec((latent, block), lambda i: (0, i)),
         ],
-        out_specs=[
-            pl.BlockSpec((rows, WIDTH), lambda i: (0, 0)),
-            pl.BlockSpec((rows, LANES), lambda i: (0, 0)),
-            pl.BlockSpec((rows, LANES), lambda i: (0, 0)),
-        ],
-        out_shape=[jax.ShapeDtypeStruct((rows, WIDTH), jnp.float32), stat, stat],
+        out_specs=pl.BlockSpec((rows, WIDTH + 2 * LANES), lambda i: (0, 0)),
+        out_shape=jax.ShapeDtypeStruct((rows, WIDTH + 2 * LANES), jnp.float32),
         compiler_params=pltpu.CompilerParams(vmem_limit_bytes=20 * 1024 * 1024),
         cost_estimate=pl.CostEstimate(
             flops=2 * rows * keys * (latent + WIDTH), bytes_accessed=4 * 1024 * 1024, transcendentals=rows * keys
@@ -91,15 +93,14 @@
     )(length, query, own, cache)
 
 
-def arrived_kernel(wide_ref, low_ref, high_ref, pages_ref, acc_in_ref, top_in_ref, total_in_ref, out_ref, acc_ref, top_ref, total_ref):
+def arrived_kernel(wide_ref, low_ref, high_ref, pages_ref, before_ref, out_ref, state_ref):
+    acc_ref, top_ref, total_ref = parts_of(state_ref)
     step = pl.program_id(0)
     rows = out_ref.shape[0]
 
     @pl.when(step == 0)
     def _():
-        acc_ref[...] = acc_in_ref[...]
-        top_ref[...] = top_in_ref[...]
-        total_ref[...] = total_in_ref[...]
+        state_ref[...] = before_ref[...]
 
     count = pages_ref.shape[0] * pages_ref.shape[1]
     block = pages_ref[...].reshape(count, pages_ref.shape[2])
@@ -142,25 +143,20 @@
     low = jnp.concatenate([rope, blank], axis=1)
     high = jnp.concatenate([blank, rope], axis=1)
     whole = lambda a: pl.BlockSpec(a.shape, lambda i: (0,) * a.ndim)
-    acc, top, total = partial
     keys = 2 * sources * page
     return pl.pallas_call(
         arrived_kernel,
         grid=(sources // block,),
-        in_specs=[whole(wide_query), whole(low), whole(high), pl.BlockSpec((block, page, wide), lambda i: (i, 0, 0)), whole(acc), whole(top), whole(total)],
+        in_specs=[whole(wide_query), whole(low), whole(high), pl.BlockSpec((block, page, wide), lambda i: (i, 0, 0)), whole(partial)],
         out_specs=pl.BlockSpec((rows, WIDTH), lambda i: (0, 0)),
         out_shape=jax.ShapeDtypeStruct((rows, WIDTH), jnp.bfloat16),
-        scratch_shapes=[
-            pltpu.VMEM((rows, WIDTH), jnp.float32),
-            pltpu.VMEM((rows, LANES), jnp.float32),
-            pltpu.VMEM((rows, LANES), jnp.float32),
-        ],
+        scratch_shapes=[pltpu.VMEM((rows, WIDTH + 2 * LANES), jnp.float32)],
         compiler_params=pltpu.CompilerParams(vmem_limit_bytes=20 * 1024 * 1024),
         cost_estimate=pl.CostEstimate(
             flops=2 * rows * keys * (2 * WIDTH + LANES), bytes_accessed=4 * 1024 * 1024, transcendentals=rows * keys
         ),
         name="arrived",
-    )(wide_query, low, high, pages, acc, top, total)
+    )(wide_query, low, high, pages, partial)
 
 
 def slots_kernel(owner_ref, pages_ref, out_ref):
@@ -223,18 +219,46 @@
     out_ref[:, rows * part :] = scratch_ref[:, 0, part:].astype(jnp.bfloat16)
 
 
-def fold_kernel(own_ref, after_ref, before_ref, out_ref, scratch_ref):
-    rows, fold, part = out_ref.shape
-    for k in range(fold):
-        columns = slice(k * part, (k + 1) * part)
-        term = own_ref[:, columns] + after_ref[:, columns].astype(jnp.float32) + before_ref[:, columns].astype(jnp.float32)
-        scratch_ref[:, k, :] = term
-    out_ref[...] = scratch_ref[...].astype(jnp.bfloat16)
-
-
-def shift(value, by):
-    count = lax.axis_size("y")
-    return lax.ppermute(value, "y", [(i, (i + by) % count) for i in range(count)])
+def fold_kernel(*refs):
+    inputs, outs, scratches = refs[:6], refs[6:14], refs[14:]
+    for half, scratch_ref in enumerate(scratches):
+        own_ref, after_ref, before_ref = inputs[3 * half : 3 * half + 3]
+        blocks = outs[4 * half : 4 * half + 4]
+        fold, part = scratch_ref.shape[1:]
+        for k in range(fold):
+            columns = slice(k * part, (k + 1) * part)
+            term = own_ref[:, columns] + after_ref[:, columns].astype(jnp.float32) + before_ref[:, columns].astype(jnp.float32)
+            scratch_ref[:, k, :] = term
+        depth = blocks[0].shape[0]
+        for place, block in enumerate(blocks):
+            block[...] = scratch_ref[place * depth : (place + 1) * depth].astype(block.dtype)
+
+
+def join_kernel(*refs):
+    blocks, out_ref = refs[:-1], refs[-1]
+    start = 0
+    for half in (blocks[:4], blocks[4:]):
+        total = half[0][...]
+        for block in half[1:]:
+            total = total + block[...].astype(jnp.float32)
+        out_ref[:, :, start : start + total.shape[2]] = total.astype(jnp.bfloat16)
+        start += total.shape[2]
+
+
+def final_kernel(ends_ref, out_ref):
+    total = jnp.sum(ends_ref[...].astype(jnp.float32), axis=0)
+    fold, wide = total.shape
+    start = 0
+    for first, last in ((0, SPLIT // fold), (SPLIT // fold, wide)):
+        part = last - first
+        for k in range(fold):
+            out_ref[:, start + k * part : start + (k + 1) * part] = total[k : k + 1, first:last].astype(jnp.bfloat16)
+        start += fold * part
+
+
+def shift(value, by, axis="y"):
+    count = lax.axis_size(axis)
+    return lax.ppermute(value, axis, [(i, (i + by) % count) for i in range(count)])
 
 
 def gather_slab(moe_input, expert_ids, gate_weights, beside):
@@ -255,40 +279,101 @@
     )(got, *beside)
 
 
-def expert_term(tokens, w_in, w_out, my_expert):
-    model = w_in.shape[0]
-    experts = lax.broadcasted_iota(jnp.int32, (1, LANES), 1)
-    row_weight = jnp.sum(jnp.where(experts == my_expert, tokens[:, model:].astype(jnp.float32), 0.0), axis=1)
-    both = dot(tokens[:, :model], w_in)
-    units = both.shape[1] // 2
+def hidden_kernel(place_ref, *refs):
+    pieces, w_ref, outs, (tokens_ref, sems) = refs[:10], refs[10], refs[11:15], refs[15:]
+    copies = []
+    start = 0
+    for number, piece in enumerate(pieces):
+        rows = piece.shape[0]
+        copies.append(pltpu.make_async_copy(piece, tokens_ref.at[pl.ds(start, rows)], sems.at[number]))
+        start += rows
+    for copy in copies:
+        copy.start()
+    for copy in copies:
+        copy.wait()
+    model, columns = w_ref.shape
+    depth = 896
+
+    def add(k, total):
+        span = pl.ds(pl.multiple_of(k * depth, LANES), depth)
+        return total + dot(tokens_ref[:, span], w_ref[span, :])
+
+    both = lax.fori_loop(0, model // depth, add, jnp.zeros((tokens_ref.shape[0], columns), jnp.float32))
+    units = columns // 2
     hidden = (jax.nn.silu(both[:, :units]) * both[:, units:]).astype(jnp.bfloat16)
-    return dot(hidden, w_out) * row_weight[:, None]
-
-
-def expert_part(tokens, *rest):
-    sent = expert_term(swap(tokens), *rest).astype(jnp.bfloat16)
-    return expert_term(tokens, *rest) + swap(sent).astype(jnp.float32)
+    expert = lax.broadcasted_iota(jnp.int32, (1, LANES), 1)
+    weight = jnp.where(expert == place_ref[0], tokens_ref[:, model:].astype(jnp.float32), 0.0)
+    weight = jnp.broadcast_to(jnp.sum(weight, axis=1, keepdims=True), weight.shape).astype(jnp.bfloat16)
+    both = jnp.concatenate([hidden, weight], axis=1)
+    count = both.shape[0] // 2
+    row = lax.broadcasted_iota(jnp.int32, (count, count), 0)
+    column = lax.broadcasted_iota(jnp.int32, (count, count), 1)
+    high, middle, low = row >> 5, (row >> 3) & 3, row & 7
+    for half, (y, x) in enumerate(((high, middle), (middle, high))):
+        offset = jnp.where(x == 1, 3, jnp.where(x == 2, 1, jnp.where(x == 3, 2, 0)))
+        source = y * 32 + ((place_ref[1] + offset) & 3) * 8 + low
+        order = jnp.where(source == column, 1.0, 0.0).astype(jnp.bfloat16)
+        outs[2 * half][...] = dot(order, both[:count]).astype(jnp.bfloat16)
+        outs[2 * half + 1][...] = dot(order, both[count:]).astype(jnp.bfloat16)
+
+
+def hidden_rows(pieces, w_in, my_expert):
+    count = 2 * sum(piece.shape[0] for piece in pieces)
+    shape = jax.ShapeDtypeStruct((count // 2, 2 * LANES), jnp.bfloat16)
+    anywhere = pl.BlockSpec(memory_space=pl.ANY)
+    return pl.pallas_call(
+        hidden_kernel,
+        in_specs=[pl.BlockSpec(memory_space=pltpu.SMEM)] + [anywhere] * 10 + [pl.BlockSpec(memory_space=pltpu.VMEM)],
+        out_shape=[shape] * 4,
+        scratch_shapes=[
+            pltpu.VMEM((count, pieces[0].shape[1]), jnp.bfloat16),
+            pltpu.SemaphoreType.DMA((10,)),
+        ],
+        compiler_params=pltpu.CompilerParams(vmem_limit_bytes=16 * 1024 * 1024),
+        cost_estimate=pl.CostEstimate(flops=2 * count * w_in.size, bytes_accessed=8 * 1024 * 1024, transcendentals=0),
+        name="hidden",
+    )(jnp.stack([my_expert, lax.axis_index("x")]).astype(jnp.int32), *pieces, *[swap(piece) for piece in pieces], w_in)
+
+
+def expert_part(hidden, other, w_out):
+    term = lambda rows: dot(rows[:, : w_out.shape[0]], w_out) * rows[:, w_out.shape[0] :][:, :1].astype(jnp.float32)
+    got = swap(term(other).astype(jnp.bfloat16))
+    return term(hidden) + got.astype(jnp.float32)
+
+
+def ring_sum(hidden, other, w_out, axis):
+    rows = hidden.shape[0] // 4
+    half = rows // 2
+    opposite = expert_part(hidden[3 * rows :], other[3 * rows :], w_out).astype(jnp.bfloat16)
+    top, bottom = shift(opposite[:half], 1, axis), shift(opposite[half:], -1, axis)
+    near = expert_part(hidden[: 3 * rows], other[: 3 * rows], w_out)
+    back = jnp.concatenate([near[rows : rows + half], near[rows + half : 2 * rows] + bottom.astype(jnp.float32)], axis=0)
+    ahead = jnp.concatenate([near[2 * rows : 2 * rows + half] + top.astype(jnp.float32), near[2 * rows + half :]], axis=0)
+    return near[:rows], shift(ahead.astype(jnp.bfloat16), 1, axis), shift(back.astype(jnp.bfloat16), -1, axis)
 
 
 def experts_sum(slab, before, after, w_in, w_out, my_expert):
+    half = slab.shape[0] // 2
+    first, second = shift(before[:half], 1), shift(after[half:], -1)
+    y_rows, y_other, x_rows, x_other = hidden_rows((slab, before, after, first, second), w_in, my_expert)
+    terms = ring_sum(y_rows, y_other, w_out[:, :SPLIT], "y") + ring_sum(x_rows, x_other, w_out[:, SPLIT:], "x")
     rows = slab.shape[0]
-    half = rows // 2
-    first, second = shift(before[:half], 1), shift(after[half:], -1)
-    near = expert_part(jnp.concatenate([before, after, slab], axis=0), w_in, w_out, my_expert)
-    far = expert_part(jnp.concatenate([first, second], axis=0), w_in, w_out, my_expert)
-    opposite = far.astype(jnp.bfloat16)
-    top, bottom = shift(opposite[:half], 1), shift(opposite[half:], -1)
-    near_before = jnp.concatenate([near[:half], near[half:rows] + bottom.astype(jnp.float32)], axis=0)
-    near_after = jnp.concatenate([near[rows : rows + half] + top.astype(jnp.float32), near[rows + half : 2 * rows]], axis=0)
-    terms = (near[2 * rows :], shift(near_after.astype(jnp.bfloat16), 1), shift(near_before.astype(jnp.bfloat16), -1))
-    folded = (rows, FOLD, far.shape[1] // FOLD)
-    return pl.pallas_call(
+    depth = rows // 4
+    parts = (SPLIT // FOLD, (w_out.shape[1] - SPLIT) // FOLD)
+    shapes = [jax.ShapeDtypeStruct((depth, FOLD, part), dtype) for part in parts for dtype in (jnp.float32,) + (jnp.bfloat16,) * 3]
+    blocks = pl.pallas_call(
         fold_kernel,
-        out_shape=jax.ShapeDtypeStruct(folded, jnp.bfloat16),
-        scratch_shapes=[pltpu.VMEM(folded, jnp.float32)],
+        out_shape=shapes,
+        scratch_shapes=[pltpu.VMEM((rows, FOLD, part), jnp.float32) for part in parts],
         compiler_params=SMALL,
         name="fold",
     )(*terms)
+    moved = []
+    for axis, group in (("x", blocks[:4]), ("y", blocks[4:])):
+        moved += [group[0]] + [shift(block, by, axis) for block, by in zip(group[1:], OFFSETS[1:])]
+    return pl.pallas_call(
+        join_kernel, out_shape=jax.ShapeDtypeStruct((depth, FOLD, sum(parts)), jnp.bfloat16), compiler_params=SMALL, name="join"
+    )(*moved)
 
 
 def local(
@@ -320,7 +405,7 @@
         partial = attend_resident(query, own, jnp.transpose(resident_cache[0]), resident_len)
 
     with jax.named_scope("tokens"):
-        slab = gather_slab(moe_input, expert_ids, gate_weights, (buffer, partial[0]))
+        slab = gather_slab(moe_input, expert_ids, gate_weights, (buffer, partial))
         before, after = shift(slab, 1), shift(slab, -1)
 
     with jax.named_scope("experts"):
@@ -337,13 +422,15 @@
             held, _ = lax.optimization_barrier(((slab, before, after), i))
             return experts_sum(*held, w_in[0], w_out[0], slice_index // group)
 
-        blank = jnp.zeros((rows, FOLD, model // FOLD), jnp.bfloat16)
+        blank = jnp.zeros((rows // 4, FOLD, model // FOLD), jnp.bfloat16)
         sums = lax.fori_loop(0, lax.optimization_barrier(jnp.int32(1)), turn, blank)
 
     with jax.named_scope("sums"):
         sums, arrived = lax.optimization_barrier((sums, arrived))
-        ends = lax.all_to_all(sums, SLAB, 0, 0, tiled=True)
-        mixed = jnp.sum(ends.astype(jnp.float32), axis=0).reshape(1, model).astype(jnp.bfloat16)
+        ends = lax.all_to_all(sums, "z", 0, 0, tiled=True)
+        mixed = pl.pallas_call(
+            final_kernel, out_shape=jax.ShapeDtypeStruct((1, model), jnp.bfloat16), compiler_params=SMALL, name="final"
+        )(ends)
 
     with jax.named_scope("attention"):
         context = attend_arrived(query, arrived, partial)

time: 133 us -> 135 us (1.015); the launches traced: 132 us -> 133 us
  starting transfers between devices: 40.3 us -> 55 us
  waiting for transfers between devices: 49.6 us -> 39.4 us
  Pallas kernels: 19.8 us -> 28.8 us
  local copies, waits for them, and re-layouts: 13.3 us -> 4.72 us
  matrix products: 4.88 us -> 2.39 us
  other arithmetic: 3.03 us -> 0.91 us
    ppermute x8 -> x18, starting transfers between devices: 9.54 us -> 23.7 us  [shift(): lax.ppermute(value, axis, [(i, (i + by) % count) for i in range(count)])]
    pallas_call x1 -> x4, Pallas kernels: 1.25 us -> 8.98 us  [the longest x1 7.2 us: hidden_rows(): pl.pallas_call(hidden_kernel, in_specs=[pl.BlockSpec(memory_space=pltpu.S...]
    all_to_all x1, waiting for transfers between devices: 9.55 us -> 3.15 us  [local(): ends = lax.all_to_all(sums, 'z', 0, 0, tiled=True)]
    ppermute x8 -> x18, waiting for transfers between devices: 35 us -> 29 us  [shift(): lax.ppermute(value, axis, [(i, (i + by) % count) for i in range(count)])]
    while x9 -> x2, local copies, waits for them, and re-layouts: 2.79 us -> 0.01 us
    dot_general x8, matrix products: 4.88 us -> 2.39 us  [dot(): return jnp.dot(a, b, preferred_element_type=jnp.float32)]
    ppermute x6 -> x11, waiting for transfers between devices: 0.41 us -> 2.69 us  [swap(): return lax.ppermute(value, 'pool', [(0, 1), (1, 0)])]
    all_to_all x1, starting transfers between devices: 9.1 us -> 7.22 us  [local(): ends = lax.all_to_all(sums, 'z', 0, 0, tiled=True)]
  transfers between devices with their start and end apart: 17 -> 32, of which waited for: 11 -> 14; matrix products, arithmetic and copies ran while one was open for 13% -> 5% of each run, Pallas kernels for 13% -> 19%
where the time goes in v3:
time: 135 us; the launch traced here: 133 us
  starting transfers between devices  55 us (41%)
  waiting for transfers between devices  39.4 us (29%)
  Pallas kernels  28.8 us (21%)
  local copies, waits for them, and re-layouts  4.72 us (3%)
  matrix products  2.39 us (2%)
  between operations  1.47 us (1%)
    ppermute x18, waiting for transfers between devices, shift(): lax.ppermute(value, axis, [(i, (i + by) % count) for i in range(count)])  29 us
    ppermute x18, starting transfers between devices, shift(): lax.ppermute(value, axis, [(i, (i + by) % count) for i in range(count)])  23.7 us
    all_to_all x1, starting transfers between devices, gather_slab(): got = lax.all_to_all(sent, SLAB, 0, 0, tiled=True)  11.3 us
    all_to_all x1, starting transfers between devices, local(): arrived = lax.all_to_all(buffer, CHIPS, 0, 0, tiled=True)  9.95 us
    all_to_all x1, starting transfers between devices, local(): ends = lax.all_to_all(sums, 'z', 0, 0, tiled=True)  7.22 us
    pallas_call x1, Pallas kernels, hidden_rows(): pl.pallas_call(hidden_kernel, in_specs=[pl.BlockSpec(memory_space=pltpu.S...  7.2 us
    pallas_call x1, Pallas kernels, slot_buffer(): pl.pallas_call(slots_kernel, out_shape=jax.ShapeDtypeStruct((peers * page...  5.73 us
    pallas_call x1, Pallas kernels, attend_arrived(): pl.pallas_call(arrived_kernel, grid=(sources // block,), in_specs=[whole(...  5.66 us
  transfers between devices with their start and end apart: 32, of which 14 were waited for; matrix products, arithmetic and copies ran while one was open for 5% of the time, Pallas kernels for 19%

profile of v3, /device:TPU:24, one launch (start us, length us, event | category | flops | bytes accessed | tf_op | source)
XLA Modules:
  0.0 133.0 jit_solution(12138600218439677683)
XLA Ops:
  0.8 1.7 %token_.1 = bf16[32,8,1024]{2,1,0:T(8,128)(2,1)} custom-call(bf16[1,7168]{1,0:T(2,128)(2,1)} %input_ref.1, s32[1,8]{1,0:T(1,128)} %ids_ref.1, bf16[1,8]{1,0:T(2,128)(2,1)} %gates_ref.1), custom_call_target="tpu_custom_call" | custom-call | tf_op jit(solution)/shard_map/tokens/token/pallas_call | solution.py:268
  2.4 11.3 %all-to-all-start = ((bf16[32,8,1024]{2,1,0:T(8,128)(2,1)}), bf16[32,8,1024]{2,1,0:T(8,128)(2,1)S(1)}, u32[]{:S(2)}, u32[]{:S(2)}) async-start(bf16[32,8,1024]{2,1,0:T(8,128)(2,1)} %token_.1), calls=%async_computation | async-start | bytes 1048576 | tf_op jit(solution)/shard_map/tokens/all_to_all | solution.py:271
  13.8 0.3 collective-permute-start.25
  14.1 0.2 copy.15
  15.0 1.7 %copy-done = bf16[1,2048,576]{1,2,0:T(8,128)(2,1)S(1)} copy-done((bf16[1,2048,576]{1,2,0:T(8,128)(2,1)S(1)}, bf16[1,2048,576]{1,2,0:T(8,128)(2,1)}, u32[]{:S(2)}) %copy-start) | copy-done | bytes 2359320
  16.6 4.2 %resident.1.partial_ref.before_ref = f32[256,768]{1,0:T(8,128)S(1)} custom-call(s32[1]{0:T(128)S(6)} %copy.24.length_ref, bf16[256,576]{1,0:T(8,128)(2,1)S(1)} %bitcast.23, bf16[16,576]{1,0:T(8,128)(2,1)S(1)} %concatenate.43.own_ref, bf16[576,2048]{1,0:T(8,128)(2,1)S(1)} %bitcast.26), custom_call_target="tpu_custom_call" | custom-call | flops 1140850688 | bytes 4194304 | tf_op jit(solution)/shard_map/resident/resident/pallas_call | solution.py:77
  20.8 5.7 %slots.1 = bf16[1024,1152]{1,0:T(8,128)(2,1)} custom-call(s32[1,128]{1,0:T(1,128)S(1)} %collective-permute-done.25.owner_ref, bf16[8,576,128]{2,1,0:T(8,128)(2,1)S(1)} %collective-permute-done.26.pages_ref), custom_call_target="tpu_custom_call" | custom-call | flops 2415919104 | bytes 4194304 | tf_op jit(solution)/shard_map/pages/slots/pallas_call | solution.py:191
  26.6 4.6 %all-to-all-done.folded_ref = bf16[32,8,1024]{2,1,0:T(8,128)(2,1)S(1)} async-done(((bf16[32,8,1024]{2,1,0:T(8,128)(2,1)}), bf16[32,8,1024]{2,1,0:T(8,128)(2,1)S(1)}, u32[]{:S(2)}, u32[]{:S(2)}) %all-to-all-start) | async-done | bytes 524320 | tf_op jit(solution)/shard_map/tokens/all_to_all | solution.py:271
  31.2 2.6 %unfold.1 = bf16[32,7296]{1,0:T(8,128)(2,1)} custom-call(bf16[32,8,1024]{2,1,0:T(8,128)(2,1)S(1)} %all-to-all-done.folded_ref, bf16[128,8,1152]{2,1,0:T(8,128)(2,1)} %bitcast.7.buffer_ref, f32[256,768]{1,0:T(8,128)S(1)} %resident.1.partial_ref.before_ref), custom_call_target="tpu_custom_call" | custom-call | tf_op jit(solution)/shard_map/tokens/unfold/pallas_call | solution.py:272
  33.7 0.2 collective-permute-start.27
  34.0 1.8 %collective-permute-start.28 = (bf16[32,7296]{1,0:T(8,128)(2,1)}, bf16[32,7296]{1,0:T(8,128)(2,1)}, u32[]{:S(2)}, u32[]{:S(2)}) collective-permute-start(bf16[32,7296]{1,0:T(8,128)(2,1)} %unfold.1), channel_id=1, source_target_pairs={{0,12},{4,0},{8,4},{12,8},{1,13},{5,1},{9,5},{13,9},{2,14},{6,2},{... | collective-permute-start | bytes 1400840 | tf_op jit(solution)/shard_map/tokens/ppermute | solution.py:261
  35.9 10.0 %all-to-all-start.1 = ((bf16[128,8,1152]{2,1,0:T(8,128)(2,1)}), bf16[128,8,1152]{2,1,0:T(8,128)(2,1)}, u32[]{:S(2)}, u32[]{:S(2)}) async-start(bf16[128,8,1152]{2,1,0:T(8,128)(2,1)} %bitcast.7.buffer_ref), calls=%async_computation.1 | async-start | bytes 4718592 | tf_op jit(solution)/shard_map/pages/all_to_all | solution.py:401
  45.9 0.7 broadcast_in_dim.2
  46.5 69.7 %while.13 = (s32[]{:T(128)}, bf16[8,8,896]{2,1,0:T(8,128)(2,1)}, s32[]{:T(128)}, s32[]{:T(128)}, bf16[32,7296]{1,0:T(8,128)(2,1)}, /*index=5*/bf16[32,7296]{1,0:...) while((s32[]{:T(128)}, bf16[8,8,896]{2,1,0:T(8,128)(2,1)}, ...), condition=%wide.region_1.2_spmd, body=%wide.region_0.1_spmd.sunk | while | flops 1417314688 | bytes 63299732 | solution.py:426
  46.5 1.0 slice.404
  47.5 1.0 collective-permute-start
  48.5 0.2 collective-permute-start.2
  48.7 0.3 collective-permute-start.4
  49.0 1.0 slice.405
  50.0 1.2 collective-permute-start.1
  51.1 11.6 %collective-permute-done.refs_3_ = bf16[16,7296]{1,0:T(8,128)(2,1)S(1)} collective-permute-done((bf16[16,7296]{1,0:T(8,128)(2,1)S(1)}, bf16[16,7296]{1,0:T(8,128)(2,1)S(1)}, u32[]{:S(2)}, u32[]{:S(2)}) %collective-permute-start) | collective-permute-done | bytes 233504 | tf_op jit(solution)/shard_map/experts/while/body/ppermute | solution.py:261
  62.8 0.5 collective-permute-start.6
  63.4 0.9 collective-permute-done.5.refs_8_
  64.3 0.3 collective-permute-done.6.refs_9_
  64.6 7.2 %hidden.4 = (bf16[128,256]{1,0:T(8,128)(2,1)S(1)}, bf16[128,256]{1,0:T(8,128)(2,1)S(1)}, bf16[128,256]{1,0:T(8,128)(2,1)S(1)}, bf16[128,256]{1,0:T(8,128)(2,1)S(1)}) custom-call(s32[2]{0:T(128)S(1)} %pad_add_fusion.2.place_ref, bf16[32,7296]{1,0:T(8,128)(2,1)} %get-tuple-element.338.refs_0_, bf16[32,7296]{1,0:T(8,128)(2,1)} %get-tuple-element.339.refs_1_, ...), custom_call_target="tpu_custom_call" | custom-call | flops 939524096 | bytes 8388608 | tf_op jit(solution)/shard_map/experts/while/body/hidden/pallas_call | solution.py:324
  71.9 0.1 convert_reduce_fusion.16
  72.0 0.1 convert_reduce_fusion.18
  72.1 0.1 convert_reduce_fusion.19
  72.3 0.4 fusion.76
  72.7 0.3 collective-permute-start.7
  72.9 0.3 fusion.79
  73.2 0.4 collective-permute-start.8
  73.6 0.3 fusion.83
  73.9 0.3 collective-permute-start.13
  74.2 0.2 fusion.86
  74.4 0.4 collective-permute-start.14
  74.9 0.1 convert_reduce_fusion.17
  75.0 0.1 convert_reduce_fusion.15
  75.1 1.4 %collective-permute-done.14 = bf16[32,3072]{1,0:T(8,128)(2,1)S(1)} collective-permute-done((bf16[32,3072]{1,0:T(8,128)(2,1)S(1)}, bf16[32,3072]{1,0:T(8,128)(2,1)S(1)}, u32[]{:S(2)}, u32[]{:S(2)}) %collective-permute-start.14) | collective-permute-done | bytes 196640 | tf_op jit(solution)/shard_map/experts/while/body/ppermute | solution.py:25
  76.5 0.2 fusion.87
  76.8 2.9 %collective-permute-start.15 = (bf16[16,3072]{1,0:T(8,128)(2,1)S(1)}, bf16[16,3072]{1,0:T(8,128)(2,1)S(1)}, u32[]{:S(2)}, u32[]{:S(2)}) collective-permute-start(bf16[16,3072]{1,0:T(8,128)(2,1)S(1)} %get-tuple-element.360), channel_id=1, source_target_pairs={{0,3},{1,0},{2,1},{3,2},{4,7},{5,4},{6,5},{7,6},{8,11},{9,8},{10,9... | collective-permute-start | bytes 294920 | tf_op jit(solution)/shard_map/experts/while/body/ppermute | solution.py:261
  79.7 0.3 fusion.80
  80.1 3.2 %collective-permute-start.10 = (bf16[16,4096]{1,0:T(8,128)(2,1)S(1)}, bf16[16,4096]{1,0:T(8,128)(2,1)S(1)}, u32[]{:S(2)}, u32[]{:S(2)}) collective-permute-start(bf16[16,4096]{1,0:T(8,128)(2,1)S(1)} %get-tuple-element.350), channel_id=1, source_target_pairs={{0,4},{4,8},{8,12},{12,0},{1,5},{5,9},{9,13},{13,1},{2,6},{6,10},{... | collective-permute-start | bytes 393224 | tf_op jit(solution)/shard_map/experts/while/body/ppermute | solution.py:261
  83.3 0.3 fusion.84
  83.7 1.1 collective-permute-done.15
  84.7 3.1 %collective-permute-done.16 = bf16[16,3072]{1,0:T(8,128)(2,1)S(1)} collective-permute-done((bf16[16,3072]{1,0:T(8,128)(2,1)S(1)}, bf16[16,3072]{1,0:T(8,128)(2,1)S(1)}, u32[]{:S(2)}, u32[]{:S(2)}) %collective-permute-start.16) | collective-permute-done | bytes 98336 | tf_op jit(solution)/shard_map/experts/while/body/ppermute | solution.py:261
  88.0 0.4 fusion.77
  88.4 0.5 collective-permute-done.9
  89.0 3.1 %collective-permute-start.11 = (bf16[32,4096]{1,0:T(8,128)(2,1)S(1)}, bf16[32,4096]{1,0:T(8,128)(2,1)S(1)}, u32[]{:S(2)}, u32[]{:S(2)}) collective-permute-start(bf16[32,4096]{1,0:T(8,128)(2,1)S(1)} %pad_maximum_fusion.9), channel_id=1, source_target_pairs={{0,4},{4,8},{8,12},{12,0},{1,5},{5,9},{9,13},{13,1},{2,6},{6,10},{... | collective-permute-start | bytes 786440 | tf_op jit(solution)/shard_map/experts/while/body/ppermute | solution.py:261
  92.2 2.7 %collective-permute-start.18 = (bf16[32,3072]{1,0:T(8,128)(2,1)S(1)}, bf16[32,3072]{1,0:T(8,128)(2,1)S(1)}, u32[]{:S(2)}, u32[]{:S(2)}) collective-permute-start(bf16[32,3072]{1,0:T(8,128)(2,1)S(1)} %pad_maximum_fusion.12), channel_id=1, source_target_pairs={{0,3},{1,0},{2,1},{3,2},{4,7},{5,4},{6,5},{7,6},{8,11},{9,8},{10,9... | collective-permute-start | bytes 589832 | tf_op jit(solution)/shard_map/experts/while/body/ppermute | solution.py:261
  95.0 3.3 %collective-permute-done.17.refs_4_ = bf16[32,3072]{1,0:T(8,128)(2,1)S(1)} collective-permute-done((bf16[32,3072]{1,0:T(8,128)(2,1)S(1)}, bf16[32,3072]{1,0:T(8,128)(2,1)S(1)}, u32[]{:S(2)}, u32[]{:S(2)}) %collective-permute-start.17) | collective-permute-done | bytes 196640 | tf_op jit(solution)/shard_map/experts/while/body/ppermute | solution.py:261
  98.3 0.6 collective-permute-done.18.refs_5_
  98.9 3.2 %collective-permute-done.12.refs_2_ = bf16[32,4096]{1,0:T(8,128)(2,1)S(1)} collective-permute-done((bf16[32,4096]{1,0:T(8,128)(2,1)S(1)}, bf16[32,4096]{1,0:T(8,128)(2,1)S(1)}, u32[]{:S(2)}, u32[]{:S(2)}) %collective-permute-start.12) | collective-permute-done | bytes 262176 | tf_op jit(solution)/shard_map/experts/while/body/ppermute | solution.py:261
  102.1 0.4 fold.4
  102.7 2.3 %collective-permute-start.19 = (bf16[8,8,512]{2,1,0:T(8,128)(2,1)S(1)}, bf16[8,8,512]{2,1,0:T(8,128)(2,1)S(1)}, u32[]{:S(2)}, u32[]{:S(2)}) collective-permute-start(bf16[8,8,512]{2,1,0:T(8,128)(2,1)S(1)} %get-tuple-element.366), channel_id=1, source_target_pairs={{0,3},{1,0},{2,1},{3,2},{4,7},{5,4},{6,5},{7,6},{8,11},{9,8},{10,9... | collective-permute-start | bytes 196616 | tf_op jit(solution)/shard_map/experts/while/body/ppermute | solution.py:261
  105.0 1.8 %collective-permute-start.21 = (bf16[8,8,512]{2,1,0:T(8,128)(2,1)S(1)}, bf16[8,8,512]{2,1,0:T(8,128)(2,1)S(1)}, u32[]{:S(2)}, u32[]{:S(2)}) collective-permute-start(bf16[8,8,512]{2,1,0:T(8,128)(2,1)S(1)} %get-tuple-element.368), channel_id=1, source_target_pairs={{0,2},{1,3},{2,0},{3,1},{4,6},{5,7},{6,4},{7,5},{8,10},{9,11},{10,... | collective-permute-start | bytes 196616 | tf_op jit(solution)/shard_map/experts/while/body/ppermute | solution.py:261
  106.8 3.1 %collective-permute-start.23 = (bf16[8,8,384]{2,1,0:T(8,128)(2,1)S(1)}, bf16[8,8,384]{2,1,0:T(8,128)(2,1)S(1)}, u32[]{:S(2)}, u32[]{:S(2)}) collective-permute-start(bf16[8,8,384]{2,1,0:T(8,128)(2,1)S(1)} %get-tuple-element.371), channel_id=1, source_target_pairs={{0,4},{4,8},{8,12},{12,0},{1,5},{5,9},{9,13},{13,1},{2,6},{6,10},{... | collective-permute-start | bytes 147464 | tf_op jit(solution)/shard_map/experts/while/body/ppermute | solution.py:261
  109.9 1.7 %collective-permute-done.23.refs_6_ = bf16[8,8,384]{2,1,0:T(8,128)(2,1)S(1)} collective-permute-done((bf16[8,8,384]{2,1,0:T(8,128)(2,1)S(1)}, bf16[8,8,384]{2,1,0:T(8,128)(2,1)S(1)}, u32[]{:S(2)}, u32[]{:S(2)}) %collective-permute-start.23) | collective-permute-done | bytes 49184 | tf_op jit(solution)/shard_map/experts/while/body/ppermute | solution.py:261
  111.6 3.8 %collective-permute-done.24.refs_7_ = bf16[8,8,384]{2,1,0:T(8,128)(2,1)S(1)} collective-permute-done((bf16[8,8,384]{2,1,0:T(8,128)(2,1)S(1)}, bf16[8,8,384]{2,1,0:T(8,128)(2,1)S(1)}, u32[]{:S(2)}, u32[]{:S(2)}) %collective-permute-start.24) | collective-permute-done | bytes 49184 | tf_op jit(solution)/shard_map/experts/while/body/ppermute | solution.py:261
  115.5 0.7 join.4
  116.2 7.2 %all-to-all-start.2 = ((bf16[8,8,896]{2,1,0:T(8,128)(2,1)}), bf16[8,8,896]{2,1,0:T(8,128)(2,1)S(1)}, u32[]{:S(2)}, u32[]{:S(2)}) async-start(bf16[8,8,896]{2,1,0:T(8,128)(2,1)} %get-tuple-element.204), calls=%async_computation.2 | async-start | bytes 229376 | tf_op jit(solution)/shard_map/sums/all_to_all | solution.py:430
  123.5 5.7 %arrived.1 = bf16[256,512]{1,0:T(8,128)(2,1)} custom-call(bf16[272,512]{1,0:T(8,128)(2,1)S(1)} %pad_maximum_fusion.4.wide_ref, bf16[256,128]{1,0:T(8,128)(2,1)S(1)} %get-tuple-element.248.low_ref, bf16[256,128]{1,0:T(8,128)(2,1)S(1)} %get-tuple-element.247.high_ref, bf16[128,8,1152]{2,1,0:T(8,128)(2,1)} %all-to-all-done.1.pages_ref, ...), custom_call_target="tpu_custom_call" | custom-call | flops 1207959552 | bytes 4194304 | tf_op jit(solution)/shard_map/attention/arrived/pallas_call | solution.py:147
  129.2 3.2 %all-to-all-done.2.ends_ref = bf16[8,8,896]{2,1,0:T(8,128)(2,1)S(1)} async-done(((bf16[8,8,896]{2,1,0:T(8,128)(2,1)}), bf16[8,8,896]{2,1,0:T(8,128)(2,1)S(1)}, u32[]{:S(2)}, u32[]{:S(2)}) %all-to-all-start.2) | async-done | bytes 114720 | tf_op jit(solution)/shard_map/sums/all_to_all | solution.py:430
  132.3 0.6 final.1
  (58 shorter events, 1.1 us)
Async XLA Ops:
  0.6 13.1 %copy-start.4 = (s32[128,1]{0,1:T(1,128)S(1)}, s32[128,1]{0,1:T(1,128)}, u32[]{:S(2)}) copy-start(s32[128,1]{0,1:T(1,128)} %param.18) | copy-start | bytes 1540
  0.6 13.4 %copy-start.2 = (bf16[2,1,128,576]{2,3,1,0:T(8,128)(2,1)S(1)}, bf16[2,1,128,576]{2,3,1,0:T(8,128)(2,1)}, u32[]{:S(2)}) copy-start(bf16[2,1,128,576]{2,3,1,0:T(8,128)(2,1)} %param.13) | copy-start | bytes 884740
  0.7 14.3 %copy-start.3 = (bf16[2,1,576]{2,0,1:T(2,128)(2,1)S(1)}, bf16[2,1,576]{2,0,1:T(2,128)(2,1)}, u32[]{:S(2)}) copy-start(bf16[2,1,576]{2,0,1:T(2,128)(2,1)} %param.14) | copy-start | bytes 6916
  0.7 20.2 %collective-permute-start.26 = (bf16[8,576,128]{2,1,0:T(8,128)(2,1)}, bf16[8,576,128]{2,1,0:T(8,128)(2,1)S(1)}, u32[]{:S(2)}, u32[]{:S(2)}) collective-permute-start(bf16[8,576,128]{2,1,0:T(8,128)(2,1)} %bitcast.37), channel_id=1, source_target_pairs={{0,128},{128,0},{1,129},{129,1},{2,130},{130,2},{3,131},{131,3},{4... | collective-permute-start | bytes 3538952 | tf_op jit(solution)/shard_map/pages/ppermute | solution.py:25
  2.4 28.7 %all-to-all-start = ((bf16[32,8,1024]{2,1,0:T(8,128)(2,1)}), bf16[32,8,1024]{2,1,0:T(8,128)(2,1)S(1)}, u32[]{:S(2)}, u32[]{:S(2)}) async-start(bf16[32,8,1024]{2,1,0:T(8,128)(2,1)} %token_.1), calls=%async_computation | async-start | bytes 1048576 | tf_op jit(solution)/shard_map/tokens/all_to_all | solution.py:271
  13.8 7.0 %collective-permute-start.25 = (s32[1,128]{1,0:T(1,128)S(1)}, s32[1,128]{1,0:T(1,128)S(1)}, u32[]{:S(2)}, u32[]{:S(2)}) collective-permute-start(s32[1,128]{1,0:T(1,128)S(1)} %bitcast.38), channel_id=1, source_target_pairs={{0,128},{128,0},{1,129},{129,1},{2,130},{130,2},{3,131},{131,3},{4... | collective-permute-start | bytes 1544 | tf_op jit(solution)/shard_map/pages/ppermute | solution.py:25
  15.0 1.7 %copy-start = (bf16[1,2048,576]{1,2,0:T(8,128)(2,1)S(1)}, bf16[1,2048,576]{1,2,0:T(8,128)(2,1)}, u32[]{:S(2)}) copy-start(bf16[1,2048,576]{1,2,0:T(8,128)(2,1)} %param.15) | copy-start | bytes 7077892
  33.7 12.1 %collective-permute-start.27 = (bf16[32,7296]{1,0:T(8,128)(2,1)}, bf16[32,7296]{1,0:T(8,128)(2,1)}, u32[]{:S(2)}, u32[]{:S(2)}) collective-permute-start(bf16[32,7296]{1,0:T(8,128)(2,1)} %unfold.1), channel_id=1, source_target_pairs={{0,4},{4,8},{8,12},{12,0},{1,5},{5,9},{9,13},{13,1},{2,6},{6,10},{... | collective-permute-start | bytes 1400840 | tf_op jit(solution)/shard_map/tokens/ppermute | solution.py:261
  34.0 11.9 %collective-permute-start.28 = (bf16[32,7296]{1,0:T(8,128)(2,1)}, bf16[32,7296]{1,0:T(8,128)(2,1)}, u32[]{:S(2)}, u32[]{:S(2)}) collective-permute-start(bf16[32,7296]{1,0:T(8,128)(2,1)} %unfold.1), channel_id=1, source_target_pairs={{0,12},{4,0},{8,4},{12,8},{1,13},{5,1},{9,5},{13,9},{2,14},{6,2},{... | collective-permute-start | bytes 1400840 | tf_op jit(solution)/shard_map/tokens/ppermute | solution.py:261
  35.9 80.3 %all-to-all-start.1 = ((bf16[128,8,1152]{2,1,0:T(8,128)(2,1)}), bf16[128,8,1152]{2,1,0:T(8,128)(2,1)}, u32[]{:S(2)}, u32[]{:S(2)}) async-start(bf16[128,8,1152]{2,1,0:T(8,128)(2,1)} %bitcast.7.buffer_ref), calls=%async_computation.1 | async-start | bytes 4718592 | tf_op jit(solution)/shard_map/pages/all_to_all | solution.py:401
  46.5 16.8 %collective-permute-start.3 = (bf16[32,7296]{1,0:T(8,128)(2,1)}, bf16[32,7296]{1,0:T(8,128)(2,1)S(1)}, u32[]{:S(2)}, u32[]{:S(2)}) collective-permute-start(bf16[32,7296]{1,0:T(8,128)(2,1)} %get-tuple-element.339.refs_1_), channel_id=1, source_target_pairs={{0,128},{128,0},{1,129},{129,1},{2,130},{130,2},{3,131},{131,3},{4... | collective-permute-start | bytes 1400840 | tf_op jit(solution)/shard_map/experts/while/body/ppermute | solution.py:25
  47.5 15.3 %collective-permute-start = (bf16[16,7296]{1,0:T(8,128)(2,1)S(1)}, bf16[16,7296]{1,0:T(8,128)(2,1)S(1)}, u32[]{:S(2)}, u32[]{:S(2)}) collective-permute-start(bf16[16,7296]{1,0:T(8,128)(2,1)S(1)} %slice.404), channel_id=1, source_target_pairs={{0,4},{4,8},{8,12},{12,0},{1,5},{5,9},{9,13},{13,1},{2,6},{6,10},{... | collective-permute-start | bytes 700424 | tf_op jit(solution)/shard_map/experts/while/body/ppermute | solution.py:261
  48.5 14.8 %collective-permute-start.2 = (bf16[32,7296]{1,0:T(8,128)(2,1)}, bf16[32,7296]{1,0:T(8,128)(2,1)S(1)}, u32[]{:S(2)}, u32[]{:S(2)}) collective-permute-start(bf16[32,7296]{1,0:T(8,128)(2,1)} %get-tuple-element.338.refs_0_), channel_id=1, source_target_pairs={{0,128},{128,0},{1,129},{129,1},{2,130},{130,2},{3,131},{131,3},{4... | collective-permute-start | bytes 1400840 | tf_op jit(solution)/shard_map/experts/while/body/ppermute | solution.py:25
  48.7 14.6 %collective-permute-start.4 = (bf16[32,7296]{1,0:T(8,128)(2,1)}, bf16[32,7296]{1,0:T(8,128)(2,1)S(1)}, u32[]{:S(2)}, u32[]{:S(2)}) collective-permute-start(bf16[32,7296]{1,0:T(8,128)(2,1)} %get-tuple-element.340.refs_2_), channel_id=1, source_target_pairs={{0,128},{128,0},{1,129},{129,1},{2,130},{130,2},{3,131},{131,3},{4... | collective-permute-start | bytes 1400840 | tf_op jit(solution)/shard_map/experts/while/body/ppermute | solution.py:25
  50.0 12.8 %collective-permute-start.1 = (bf16[16,7296]{1,0:T(8,128)(2,1)S(1)}, bf16[16,7296]{1,0:T(8,128)(2,1)S(1)}, u32[]{:S(2)}, u32[]{:S(2)}) collective-permute-start(bf16[16,7296]{1,0:T(8,128)(2,1)S(1)} %slice.405), channel_id=1, source_target_pairs={{0,12},{4,0},{8,4},{12,8},{1,13},{5,1},{9,5},{13,9},{2,14},{6,2},{... | collective-permute-start | bytes 700424 | tf_op jit(solution)/shard_map/experts/while/body/ppermute | solution.py:261
  62.8 1.5 %collective-permute-start.5 = (bf16[16,7296]{1,0:T(8,128)(2,1)S(1)}, bf16[16,7296]{1,0:T(8,128)(2,1)S(1)}, u32[]{:S(2)}, u32[]{:S(2)}) collective-permute-start(bf16[16,7296]{1,0:T(8,128)(2,1)S(1)} %collective-permute-done.refs_3_), channel_id=1, source_target_pairs={{0,128},{128,0},{1,129},{129,1},{2,130},{130,2},{3,131},{131,3},{4... | collective-permute-start | bytes 700424 | tf_op jit(solution)/shard_map/experts/while/body/ppermute | solution.py:25
  62.8 1.8 %collective-permute-start.6 = (bf16[16,7296]{1,0:T(8,128)(2,1)S(1)}, bf16[16,7296]{1,0:T(8,128)(2,1)S(1)}, u32[]{:S(2)}, u32[]{:S(2)}) collective-permute-start(bf16[16,7296]{1,0:T(8,128)(2,1)S(1)} %collective-permute-done.1.refs_4_), channel_id=1, source_target_pairs={{0,128},{128,0},{1,129},{129,1},{2,130},{130,2},{3,131},{131,3},{4... | collective-permute-start | bytes 700424 | tf_op jit(solution)/shard_map/experts/while/body/ppermute | solution.py:25
  64.6 7.7 %copy-start.1 = (bf16[1,128,7168]{2,1,0:T(8,128)(2,1)S(1)}, bf16[1,128,7168]{2,1,0:T(8,128)(2,1)}, u32[]{:S(2)}) copy-start(bf16[1,128,7168]{2,1,0:T(8,128)(2,1)} %get-tuple-element.403) | copy-start | bytes 5505028 | tf_op jit(solution)/shard_map/experts/while
  72.7 15.3 %collective-permute-start.7 = (bf16[96,4096]{1,0:T(8,128)(2,1)S(1)}, bf16[96,4096]{1,0:T(8,128)(2,1)S(1)}, u32[]{:S(2)}, u32[]{:S(2)}) collective-permute-start(bf16[96,4096]{1,0:T(8,128)(2,1)S(1)} %fusion.76), channel_id=1, source_target_pairs={{0,128},{128,0},{1,129},{129,1},{2,130},{130,2},{3,131},{131,3},{4... | collective-permute-start | bytes 2359304 | tf_op jit(solution)/shard_map/experts/while/body/ppermute | solution.py:25
  73.2 6.5 %collective-permute-start.8 = (bf16[32,4096]{1,0:T(8,128)(2,1)S(1)}, bf16[32,4096]{1,0:T(8,128)(2,1)S(1)}, u32[]{:S(2)}, u32[]{:S(2)}) collective-permute-start(bf16[32,4096]{1,0:T(8,128)(2,1)S(1)} %fusion.79), channel_id=1, source_target_pairs={{0,128},{128,0},{1,129},{129,1},{2,130},{130,2},{3,131},{131,3},{4... | collective-permute-start | bytes 786440 | tf_op jit(solution)/shard_map/experts/while/body/ppermute | solution.py:25
  73.9 6.2 %collective-permute-start.13 = (bf16[96,3072]{1,0:T(8,128)(2,1)S(1)}, bf16[96,3072]{1,0:T(8,128)(2,1)S(1)}, u32[]{:S(2)}, u32[]{:S(2)}) collective-permute-start(bf16[96,3072]{1,0:T(8,128)(2,1)S(1)} %fusion.83), channel_id=1, source_target_pairs={{0,128},{128,0},{1,129},{129,1},{2,130},{130,2},{3,131},{131,3},{4... | collective-permute-start | bytes 1769480 | tf_op jit(solution)/shard_map/experts/while/body/ppermute | solution.py:25
  74.4 2.1 %collective-permute-start.14 = (bf16[32,3072]{1,0:T(8,128)(2,1)S(1)}, bf16[32,3072]{1,0:T(8,128)(2,1)S(1)}, u32[]{:S(2)}, u32[]{:S(2)}) collective-permute-start(bf16[32,3072]{1,0:T(8,128)(2,1)S(1)} %fusion.86), channel_id=1, source_target_pairs={{0,128},{128,0},{1,129},{129,1},{2,130},{130,2},{3,131},{131,3},{4... | collective-permute-start | bytes 589832 | tf_op jit(solution)/shard_map/experts/while/body/ppermute | solution.py:25
  76.8 7.9 %collective-permute-start.15 = (bf16[16,3072]{1,0:T(8,128)(2,1)S(1)}, bf16[16,3072]{1,0:T(8,128)(2,1)S(1)}, u32[]{:S(2)}, u32[]{:S(2)}) collective-permute-start(bf16[16,3072]{1,0:T(8,128)(2,1)S(1)} %get-tuple-element.360), channel_id=1, source_target_pairs={{0,3},{1,0},{2,1},{3,2},{4,7},{5,4},{6,5},{7,6},{8,11},{9,8},{10,9... | collective-permute-start | bytes 294920 | tf_op jit(solution)/shard_map/experts/while/body/ppermute | solution.py:261
  79.7 8.1 %collective-permute-start.16 = (bf16[16,3072]{1,0:T(8,128)(2,1)S(1)}, bf16[16,3072]{1,0:T(8,128)(2,1)S(1)}, u32[]{:S(2)}, u32[]{:S(2)}) collective-permute-start(bf16[16,3072]{1,0:T(8,128)(2,1)S(1)} %get-tuple-element.361), channel_id=1, source_target_pairs={{0,1},{1,2},{2,3},{3,0},{4,5},{5,6},{6,7},{7,4},{8,9},{9,10},{10,1... | collective-permute-start | bytes 294920 | tf_op jit(solution)/shard_map/experts/while/body/ppermute | solution.py:261
  80.0 8.9 %collective-permute-start.9 = (bf16[16,4096]{1,0:T(8,128)(2,1)S(1)}, bf16[16,4096]{1,0:T(8,128)(2,1)S(1)}, u32[]{:S(2)}, u32[]{:S(2)}) collective-permute-start(bf16[16,4096]{1,0:T(8,128)(2,1)S(1)} %get-tuple-element.349), channel_id=1, source_target_pairs={{0,12},{4,0},{8,4},{12,8},{1,13},{5,1},{9,5},{13,9},{2,14},{6,2},{... | collective-permute-start | bytes 393224 | tf_op jit(solution)/shard_map/experts/while/body/ppermute | solution.py:261
  80.1 8.8 %collective-permute-start.10 = (bf16[16,4096]{1,0:T(8,128)(2,1)S(1)}, bf16[16,4096]{1,0:T(8,128)(2,1)S(1)}, u32[]{:S(2)}, u32[]{:S(2)}) collective-permute-start(bf16[16,4096]{1,0:T(8,128)(2,1)S(1)} %get-tuple-element.350), channel_id=1, source_target_pairs={{0,4},{4,8},{8,12},{12,0},{1,5},{5,9},{9,13},{13,1},{2,6},{6,10},{... | collective-permute-start | bytes 393224 | tf_op jit(solution)/shard_map/experts/while/body/ppermute | solution.py:261
  87.9 10.4 %collective-permute-start.17 = (bf16[32,3072]{1,0:T(8,128)(2,1)S(1)}, bf16[32,3072]{1,0:T(8,128)(2,1)S(1)}, u32[]{:S(2)}, u32[]{:S(2)}) collective-permute-start(bf16[32,3072]{1,0:T(8,128)(2,1)S(1)} %pad_maximum_fusion.11), channel_id=1, source_target_pairs={{0,1},{1,2},{2,3},{3,0},{4,5},{5,6},{6,7},{7,4},{8,9},{9,10},{10,1... | collective-permute-start | bytes 589832 | tf_op jit(solution)/shard_map/experts/while/body/ppermute | solution.py:261
  89.0 9.9 %collective-permute-start.11 = (bf16[32,4096]{1,0:T(8,128)(2,1)S(1)}, bf16[32,4096]{1,0:T(8,128)(2,1)S(1)}, u32[]{:S(2)}, u32[]{:S(2)}) collective-permute-start(bf16[32,4096]{1,0:T(8,128)(2,1)S(1)} %pad_maximum_fusion.9), channel_id=1, source_target_pairs={{0,4},{4,8},{8,12},{12,0},{1,5},{5,9},{9,13},{13,1},{2,6},{6,10},{... | collective-permute-start | bytes 786440 | tf_op jit(solution)/shard_map/experts/while/body/ppermute | solution.py:261
  92.1 10.0 %collective-permute-start.12 = (bf16[32,4096]{1,0:T(8,128)(2,1)S(1)}, bf16[32,4096]{1,0:T(8,128)(2,1)S(1)}, u32[]{:S(2)}, u32[]{:S(2)}) collective-permute-start(bf16[32,4096]{1,0:T(8,128)(2,1)S(1)} %pad_maximum_fusion.10), channel_id=1, source_target_pairs={{0,12},{4,0},{8,4},{12,8},{1,13},{5,1},{9,5},{13,9},{2,14},{6,2},{... | collective-permute-start | bytes 786440 | tf_op jit(solution)/shard_map/experts/while/body/ppermute | solution.py:261
  92.2 6.6 %collective-permute-start.18 = (bf16[32,3072]{1,0:T(8,128)(2,1)S(1)}, bf16[32,3072]{1,0:T(8,128)(2,1)S(1)}, u32[]{:S(2)}, u32[]{:S(2)}) collective-permute-start(bf16[32,3072]{1,0:T(8,128)(2,1)S(1)} %pad_maximum_fusion.12), channel_id=1, source_target_pairs={{0,3},{1,0},{2,1},{3,2},{4,7},{5,4},{6,5},{7,6},{8,11},{9,8},{10,9... | collective-permute-start | bytes 589832 | tf_op jit(solution)/shard_map/experts/while/body/ppermute | solution.py:261
  102.6 7.3 %collective-permute-start.22 = (bf16[8,8,384]{2,1,0:T(8,128)(2,1)S(1)}, bf16[8,8,384]{2,1,0:T(8,128)(2,1)S(1)}, u32[]{:S(2)}, u32[]{:S(2)}) collective-permute-start(bf16[8,8,384]{2,1,0:T(8,128)(2,1)S(1)} %get-tuple-element.370), channel_id=1, source_target_pairs={{0,12},{4,0},{8,4},{12,8},{1,13},{5,1},{9,5},{13,9},{2,14},{6,2},{... | collective-permute-start | bytes 147464 | tf_op jit(solution)/shard_map/experts/while/body/ppermute | solution.py:261
  102.7 12.8 %collective-permute-start.19 = (bf16[8,8,512]{2,1,0:T(8,128)(2,1)S(1)}, bf16[8,8,512]{2,1,0:T(8,128)(2,1)S(1)}, u32[]{:S(2)}, u32[]{:S(2)}) collective-permute-start(bf16[8,8,512]{2,1,0:T(8,128)(2,1)S(1)} %get-tuple-element.366), channel_id=1, source_target_pairs={{0,3},{1,0},{2,1},{3,2},{4,7},{5,4},{6,5},{7,6},{8,11},{9,8},{10,9... | collective-permute-start | bytes 196616 | tf_op jit(solution)/shard_map/experts/while/body/ppermute | solution.py:261
  105.0 10.5 %collective-permute-start.20 = (bf16[8,8,512]{2,1,0:T(8,128)(2,1)S(1)}, bf16[8,8,512]{2,1,0:T(8,128)(2,1)S(1)}, u32[]{:S(2)}, u32[]{:S(2)}) collective-permute-start(bf16[8,8,512]{2,1,0:T(8,128)(2,1)S(1)} %get-tuple-element.367), channel_id=1, source_target_pairs={{0,1},{1,2},{2,3},{3,0},{4,5},{5,6},{6,7},{7,4},{8,9},{9,10},{10,1... | collective-permute-start | bytes 196616 | tf_op jit(solution)/shard_map/experts/while/body/ppermute | solution.py:261
  105.0 10.5 %collective-permute-start.21 = (bf16[8,8,512]{2,1,0:T(8,128)(2,1)S(1)}, bf16[8,8,512]{2,1,0:T(8,128)(2,1)S(1)}, u32[]{:S(2)}, u32[]{:S(2)}) collective-permute-start(bf16[8,8,512]{2,1,0:T(8,128)(2,1)S(1)} %get-tuple-element.368), channel_id=1, source_target_pairs={{0,2},{1,3},{2,0},{3,1},{4,6},{5,7},{6,4},{7,5},{8,10},{9,11},{10,... | collective-permute-start | bytes 196616 | tf_op jit(solution)/shard_map/experts/while/body/ppermute | solution.py:261
  106.8 4.9 %collective-permute-start.23 = (bf16[8,8,384]{2,1,0:T(8,128)(2,1)S(1)}, bf16[8,8,384]{2,1,0:T(8,128)(2,1)S(1)}, u32[]{:S(2)}, u32[]{:S(2)}) collective-permute-start(bf16[8,8,384]{2,1,0:T(8,128)(2,1)S(1)} %get-tuple-element.371), channel_id=1, source_target_pairs={{0,4},{4,8},{8,12},{12,0},{1,5},{5,9},{9,13},{13,1},{2,6},{6,10},{... | collective-permute-start | bytes 147464 | tf_op jit(solution)/shard_map/experts/while/body/ppermute | solution.py:261
  109.9 5.6 %collective-permute-start.24 = (bf16[8,8,384]{2,1,0:T(8,128)(2,1)S(1)}, bf16[8,8,384]{2,1,0:T(8,128)(2,1)S(1)}, u32[]{:S(2)}, u32[]{:S(2)}) collective-permute-start(bf16[8,8,384]{2,1,0:T(8,128)(2,1)S(1)} %get-tuple-element.372), channel_id=1, source_target_pairs={{0,8},{4,12},{8,0},{12,4},{1,9},{5,13},{9,1},{13,5},{2,10},{6,14},... | collective-permute-start | bytes 147464 | tf_op jit(solution)/shard_map/experts/while/body/ppermute | solution.py:261
  116.2 16.1 %all-to-all-start.2 = ((bf16[8,8,896]{2,1,0:T(8,128)(2,1)}), bf16[8,8,896]{2,1,0:T(8,128)(2,1)S(1)}, u32[]{:S(2)}, u32[]{:S(2)}) async-start(bf16[8,8,896]{2,1,0:T(8,128)(2,1)} %get-tuple-element.204), calls=%async_computation.2 | async-start | bytes 229376 | tf_op jit(solution)/shard_map/sums/all_to_all | solution.py:430

commit v4 on v2

--- a/solution.py
+++ b/solution.py
@@ -223,12 +223,15 @@
     out_ref[:, rows * part :] = scratch_ref[:, 0, part:].astype(jnp.bfloat16)
 
 
-def fold_kernel(own_ref, after_ref, before_ref, out_ref, scratch_ref):
+def fold_kernel(own_ref, late_after_ref, early_after_ref, early_before_ref, late_before_ref, out_ref, scratch_ref):
     rows, fold, part = out_ref.shape
+    half = rows // 2
+    pairs = ((0, late_after_ref, early_before_ref), (half, early_after_ref, late_before_ref))
     for k in range(fold):
         columns = slice(k * part, (k + 1) * part)
-        term = own_ref[:, columns] + after_ref[:, columns].astype(jnp.float32) + before_ref[:, columns].astype(jnp.float32)
-        scratch_ref[:, k, :] = term
+        for start, one, other in pairs:
+            term = one[:, columns].astype(jnp.float32) + other[:, columns].astype(jnp.float32)
+            scratch_ref[start : start + half, k, :] = own_ref[start : start + half, columns] + term
     out_ref[...] = scratch_ref[...].astype(jnp.bfloat16)
 
 
@@ -278,9 +281,11 @@
     far = expert_part(jnp.concatenate([first, second], axis=0), w_in, w_out, my_expert)
     opposite = far.astype(jnp.bfloat16)
     top, bottom = shift(opposite[:half], 1), shift(opposite[half:], -1)
-    near_before = jnp.concatenate([near[:half], near[half:rows] + bottom.astype(jnp.float32)], axis=0)
-    near_after = jnp.concatenate([near[rows : rows + half] + top.astype(jnp.float32), near[rows + half : 2 * rows]], axis=0)
-    terms = (near[2 * rows :], shift(near_after.astype(jnp.bfloat16), 1), shift(near_before.astype(jnp.bfloat16), -1))
+    low = jnp.bfloat16
+    early_after, early_before = shift(near[rows + half : 2 * rows].astype(low), 1), shift(near[:half].astype(low), -1)
+    late_after = shift((near[rows : rows + half] + top.astype(jnp.float32)).astype(low), 1)
+    late_before = shift((near[half:rows] + bottom.astype(jnp.float32)).astype(low), -1)
+    terms = (near[2 * rows :], late_after, early_after, early_before, late_before)
     folded = (rows, FOLD, far.shape[1] // FOLD)
     return pl.pallas_call(
         fold_kernel,

time: 133 us -> 133 us (level)
  waiting for transfers between devices: 49.6 us -> 44.2 us
  starting transfers between devices: 40.3 us -> 44.5 us
    ppermute x8 -> x10, waiting for transfers between devices: 35 us -> 29.1 us  [shift(): lax.ppermute(value, 'y', [(i, (i + by) % count) for i in range(count)])]
    ppermute x8 -> x10, starting transfers between devices: 9.54 us -> 14 us  [shift(): lax.ppermute(value, 'y', [(i, (i + by) % count) for i in range(count)])]
    concatenate x2 -> x0, other arithmetic: 1.6 us -> none  [the longest x1 0.81 us: experts_sum(): jnp.concatenate([near[:half], near[half:rows] + bottom.astype(jnp.float32...]
  transfers between devices with their start and end apart: 17 -> 19, of which waited for: 11 -> 11; matrix products, arithmetic and copies ran while one was open for 13% -> 13% of each run, Pallas kernels for 13% -> 13%
where the time goes in v4:
time: 133 us; the launch traced here: 131 us
  starting transfers between devices  44.5 us (33%)
  waiting for transfers between devices  44.2 us (33%)
  Pallas kernels  19.8 us (15%)
  local copies, waits for them, and re-layouts  14.1 us (11%)
  matrix products  4.88 us (4%)
  other arithmetic  2.19 us (2%)
  between operations  1.44 us (1%)
    ppermute x10, waiting for transfers between devices, shift(): lax.ppermute(value, 'y', [(i, (i + by) % count) for i in range(count)])  29.1 us
    ppermute x10, starting transfers between devices, shift(): lax.ppermute(value, 'y', [(i, (i + by) % count) for i in range(count)])  14 us
    all_to_all x1, starting transfers between devices, gather_slab(): got = lax.all_to_all(sent, SLAB, 0, 0, tiled=True)  11.3 us
    all_to_all x1, waiting for transfers between devices, local(): ends = lax.all_to_all(sums, SLAB, 0, 0, tiled=True)  10.1 us
    all_to_all x1, starting transfers between devices, local(): ends = lax.all_to_all(sums, SLAB, 0, 0, tiled=True)  8.87 us
    all_to_all x1, starting transfers between devices, local(): arrived = lax.all_to_all(buffer, CHIPS, 0, 0, tiled=True)  8.79 us
    pallas_call x1, Pallas kernels, slot_buffer(): pl.pallas_call(slots_kernel, out_shape=jax.ShapeDtypeStruct((peers * page...  5.74 us
    dot_general x8, matrix products, dot(): return jnp.dot(a, b, preferred_element_type=jnp.float32)  4.88 us
  transfers between devices with their start and end apart: 19, of which 11 were waited for; matrix products, arithmetic and copies ran while one was open for 13% of the time, Pallas kernels for 13%

profile of v4, /device:TPU:24, one launch (start us, length us, event | category | flops | bytes accessed | tf_op | source)
XLA Modules:
  0.0 131.2 jit_solution(17715404759901336607)
XLA Ops:
  0.6 0.1 collective-permute-start.13
  0.7 1.7 %token_.1 = bf16[32,8,1024]{2,1,0:T(8,128)(2,1)} custom-call(bf16[1,7168]{1,0:T(2,128)(2,1)} %input_ref.1, s32[1,8]{1,0:T(1,128)} %ids_ref.1, bf16[1,8]{1,0:T(2,128)(2,1)} %gates_ref.1), custom_call_target="tpu_custom_call" | custom-call | tf_op jit(solution)/shard_map/tokens/token/pallas_call | solution.py:247
  2.4 11.3 %all-to-all-start = ((bf16[32,8,1024]{2,1,0:T(8,128)(2,1)}), bf16[32,8,1024]{2,1,0:T(8,128)(2,1)S(1)}, u32[]{:S(2)}, u32[]{:S(2)}) async-start(bf16[32,8,1024]{2,1,0:T(8,128)(2,1)} %token_.1), calls=%async_computation | async-start | bytes 1048576 | tf_op jit(solution)/shard_map/tokens/all_to_all | solution.py:250
  13.8 0.3 collective-permute-start.12
  14.1 1.2 copy.13
  15.9 0.0 copy-start.3
  15.9 1.7 %copy-done.3 = bf16[1,2048,576]{1,2,0:T(8,128)(2,1)S(1)} copy-done((bf16[1,2048,576]{1,2,0:T(8,128)(2,1)S(1)}, bf16[1,2048,576]{1,2,0:T(8,128)(2,1)}, u32[]{:S(2)}) %copy-start.3) | copy-done | bytes 2359320
  17.6 4.2 %resident.1 = (f32[256,512]{1,0:T(8,128)S(1)}, f32[256,128]{1,0:T(8,128)S(1)}, f32[256,128]{1,0:T(8,128)S(1)}) custom-call(s32[1]{0:T(128)S(6)} %copy.26.length_ref, bf16[256,576]{1,0:T(8,128)(2,1)S(1)} %bitcast.58, bf16[16,576]{1,0:T(8,128)(2,1)S(1)} %concatenate.27.own_ref, bf16[576,2048]{1,0:T(8,128)(2,1)S(1)} %bitcast.61), custom_call_target="tpu_custom_call" | custom-call | flops 1140850688 | bytes 4194304 | tf_op jit(solution)/shard_map/resident/resident/pallas_call | solution.py:71
  21.8 5.7 %slots.1 = bf16[1024,1152]{1,0:T(8,128)(2,1)} custom-call(s32[1,128]{1,0:T(1,128)S(1)} %collective-permute-done.12.owner_ref, bf16[8,576,128]{2,1,0:T(8,128)(2,1)S(1)} %collective-permute-done.13.pages_ref), custom_call_target="tpu_custom_call" | custom-call | flops 2415919104 | bytes 4194304 | tf_op jit(solution)/shard_map/pages/slots/pallas_call | solution.py:195
  27.5 4.6 %all-to-all-done.folded_ref = bf16[32,8,1024]{2,1,0:T(8,128)(2,1)S(1)} async-done(((bf16[32,8,1024]{2,1,0:T(8,128)(2,1)}), bf16[32,8,1024]{2,1,0:T(8,128)(2,1)S(1)}, u32[]{:S(2)}, u32[]{:S(2)}) %all-to-all-start) | async-done | bytes 524320 | tf_op jit(solution)/shard_map/tokens/all_to_all | solution.py:250
  32.1 2.6 %unfold.1 = bf16[32,7296]{1,0:T(8,128)(2,1)} custom-call(bf16[32,8,1024]{2,1,0:T(8,128)(2,1)S(1)} %all-to-all-done.folded_ref, bf16[128,8,1152]{2,1,0:T(8,128)(2,1)} %bitcast.5.buffer_ref, f32[256,512]{1,0:T(8,128)S(1)} %get-tuple-element.193.partial_ref.acc_in_ref), custom_call_target="tpu_custom_call" | custom-call | tf_op jit(solution)/shard_map/tokens/unfold/pallas_call | solution.py:251
  34.7 0.2 collective-permute-start.14
  34.9 1.8 %collective-permute-start.15 = (bf16[32,7296]{1,0:T(8,128)(2,1)}, bf16[32,7296]{1,0:T(8,128)(2,1)}, u32[]{:S(2)}, u32[]{:S(2)}) collective-permute-start(bf16[32,7296]{1,0:T(8,128)(2,1)} %unfold.1), channel_id=1, source_target_pairs={{0,12},{4,0},{8,4},{12,8},{1,13},{5,1},{9,5},{13,9},{2,14},{6,2},{... | collective-permute-start | bytes 1400840 | tf_op jit(solution)/shard_map/tokens/ppermute | solution.py:240
  36.7 8.8 %all-to-all-start.1 = ((bf16[128,8,1152]{2,1,0:T(8,128)(2,1)}), bf16[128,8,1152]{2,1,0:T(8,128)(2,1)S(1)}, u32[]{:S(2)}, u32[]{:S(2)}) async-start(bf16[128,8,1152]{2,1,0:T(8,128)(2,1)} %bitcast.5.buffer_ref), calls=%async_computation.1 | async-start | bytes 4718592 | tf_op jit(solution)/shard_map/pages/all_to_all | solution.py:321
  45.5 0.9 collective-permute-done.14
  46.4 2.3 %collective-permute-done.15 = bf16[32,7296]{1,0:T(8,128)(2,1)} collective-permute-done((bf16[32,7296]{1,0:T(8,128)(2,1)}, bf16[32,7296]{1,0:T(8,128)(2,1)}, u32[]{:S(2)}, u32[]{:S(2)}) %collective-permute-start.15) | collective-permute-done | bytes 466976 | tf_op jit(solution)/shard_map/tokens/ppermute | solution.py:240
  48.7 0.8 broadcast_in_dim.54
  49.5 54.7 %while.13 = (s32[]{:T(128)}, bf16[32,8,896]{2,1,0:T(8,128)(2,1)}, s32[]{:T(128)}, bf16[32,7296]{1,0:T(8,128)(2,1)}, bf16[32,7296]{1,0:T(8,128)(2,1)}, /*index=5*...) while((s32[]{:T(128)}, bf16[32,8,896]{2,1,0:T(8,128)(2,1)}, ...), condition=%wide.region_5.6_spmd, body=%wide.region_0.5_spmd.sunk | while | flops 1415774080 | bytes 99929112 | solution.py:346
  49.5 1.0 slice.282
  50.4 0.1 collective-permute-start.2
  50.5 1.0 slice.283
  51.5 2.1 %collective-permute-start.3 = (bf16[16,7296]{1,0:T(8,128)(2,1)S(1)}, bf16[16,7296]{1,0:T(8,128)(2,1)S(1)}, u32[]{:S(2)}, u32[]{:S(2)}) collective-permute-start(bf16[16,7296]{1,0:T(8,128)(2,1)S(1)} %slice.283), channel_id=1, source_target_pairs={{0,12},{4,0},{8,4},{12,8},{1,13},{5,1},{9,5},{13,9},{2,14},{6,2},{... | collective-permute-start | bytes 700424 | tf_op jit(solution)/shard_map/experts/while/body/ppermute | solution.py:240
  53.6 1.1 constant_dynamic-update-slice_fusion.10
  54.7 1.1 constant_dynamic-update-slice_fusion.11
  55.7 6.0 %collective-permute-done.2 = bf16[16,7296]{1,0:T(8,128)(2,1)S(1)} collective-permute-done((bf16[16,7296]{1,0:T(8,128)(2,1)S(1)}, bf16[16,7296]{1,0:T(8,128)(2,1)S(1)}, u32[]{:S(2)}, u32[]{:S(2)}) %collective-permute-start.2) | collective-permute-done | bytes 233504 | tf_op jit(solution)/shard_map/experts/while/body/ppermute | solution.py:240
  61.8 0.1 collective-permute-start.4
  61.9 1.1 constant_dynamic-update-slice_fusion.12
  62.9 0.6 collective-permute-start
  63.5 0.2 collective-permute-done.4
  63.7 0.7 fusion.92
  64.4 0.1 select_reduce_fusion.7
  64.5 0.6 copy-done.5
  65.2 0.4 multiply_convert_fusion.5
  65.6 0.2 collective-permute-start.5
  65.8 0.7 fusion.90
  66.5 0.7 fusion.93
  67.2 0.2 collective-permute-done.5
  67.5 0.4 add_convert_fusion.2
  67.9 0.1 select_reduce_fusion.6
  68.0 0.8 fusion.89
  68.7 0.5 multiply_convert_fusion.4
  69.3 0.2 collective-permute-start.1
  69.6 0.6 collective-permute-start.6
  70.2 2.7 %collective-permute-start.7 = (bf16[16,7168]{1,0:T(8,128)(2,1)S(1)}, bf16[16,7168]{1,0:T(8,128)(2,1)S(1)}, u32[]{:S(2)}, u32[]{:S(2)}) collective-permute-start(bf16[16,7168]{1,0:T(8,128)(2,1)S(1)} %get-tuple-element.311), channel_id=1, source_target_pairs={{0,4},{4,8},{8,12},{12,0},{1,5},{5,9},{9,13},{13,1},{2,6},{6,10},{... | collective-permute-start | bytes 688136 | tf_op jit(solution)/shard_map/experts/while/body/ppermute | solution.py:240
  72.9 0.7 fusion.91
  73.6 8.6 %collective-permute-done.6 = bf16[16,7168]{1,0:T(8,128)(2,1)S(1)} collective-permute-done((bf16[16,7168]{1,0:T(8,128)(2,1)S(1)}, bf16[16,7168]{1,0:T(8,128)(2,1)S(1)}, u32[]{:S(2)}, u32[]{:S(2)}) %collective-permute-start.6) | collective-permute-done | bytes 229408 | tf_op jit(solution)/shard_map/experts/while/body/ppermute | solution.py:240
  82.1 0.8 collective-permute-done.7
  82.9 0.8 fusion.95
  83.7 0.8 collective-permute-start.11
  84.5 2.5 %collective-permute-start.8 = (bf16[16,7168]{1,0:T(8,128)(2,1)}, bf16[16,7168]{1,0:T(8,128)(2,1)S(1)}, u32[]{:S(2)}, u32[]{:S(2)}) collective-permute-start(bf16[16,7168]{1,0:T(8,128)(2,1)} %get-tuple-element.312), channel_id=1, source_target_pairs={{0,4},{4,8},{8,12},{12,0},{1,5},{5,9},{9,13},{13,1},{2,6},{6,10},{... | collective-permute-start | bytes 688136 | tf_op jit(solution)/shard_map/experts/while/body/ppermute | solution.py:240
  87.0 0.9 fusion.96
  87.8 3.2 %collective-permute-start.9 = (bf16[16,7168]{1,0:T(8,128)(2,1)}, bf16[16,7168]{1,0:T(8,128)(2,1)S(1)}, u32[]{:S(2)}, u32[]{:S(2)}) collective-permute-start(bf16[16,7168]{1,0:T(8,128)(2,1)} %get-tuple-element.314), channel_id=1, source_target_pairs={{0,4},{4,8},{8,12},{12,0},{1,5},{5,9},{9,13},{13,1},{2,6},{6,10},{... | collective-permute-start | bytes 688136 | tf_op jit(solution)/shard_map/experts/while/body/ppermute | solution.py:240
  91.1 1.2 slice.281.own_ref
  92.3 5.9 %collective-permute-done.11.late_before_ref = bf16[16,7168]{1,0:T(8,128)(2,1)S(1)} collective-permute-done((bf16[16,7168]{1,0:T(8,128)(2,1)}, bf16[16,7168]{1,0:T(8,128)(2,1)S(1)}, u32[]{:S(2)}, u32[]{:S(2)}) %collective-permute-start.11) | collective-permute-done | bytes 229408 | tf_op jit(solution)/shard_map/experts/while/body/ppermute | solution.py:240
  98.2 4.8 %collective-permute-done.10.early_before_ref = bf16[16,7168]{1,0:T(8,128)(2,1)S(1)} collective-permute-done((bf16[16,7168]{1,0:T(8,128)(2,1)}, bf16[16,7168]{1,0:T(8,128)(2,1)S(1)}, u32[]{:S(2)}, u32[]{:S(2)}) %collective-permute-start.10) | collective-permute-done | bytes 229408 | tf_op jit(solution)/shard_map/experts/while/body/ppermute | solution.py:240
  103.0 1.2 fold.4
  104.2 8.9 %all-to-all-start.2 = ((bf16[32,8,896]{2,1,0:T(8,128)(2,1)}), bf16[32,8,896]{2,1,0:T(8,128)(2,1)}, u32[]{:S(2)}, u32[]{:S(2)}) async-start(bf16[32,8,896]{2,1,0:T(8,128)(2,1)} %get-tuple-element.198), calls=%async_computation.2 | async-start | bytes 917504 | tf_op jit(solution)/shard_map/sums/all_to_all | solution.py:350
  113.1 0.8 slice.181
  113.9 1.0 slice.180
  114.9 0.1 fusion.52
  115.0 4.4 %arrived.1 = bf16[256,512]{1,0:T(8,128)(2,1)} custom-call(bf16[272,512]{1,0:T(8,128)(2,1)S(1)} %pad_maximum_fusion.wide_ref, bf16[256,128]{1,0:T(8,128)(2,1)S(1)} %get-tuple-element.232.low_ref, bf16[256,128]{1,0:T(8,128)(2,1)S(1)} %get-tuple-element.231.high_ref, bf16[128,8,1152]{2,1,0:T(8,128)(2,1)S(1)} %all-to-all-done.1.pages_ref, ...), custom_call_target="tpu_custom_call" | custom-call | flops 1207959552 | bytes 4194304 | tf_op jit(solution)/shard_map/attention/arrived/pallas_call | solution.py:147
  119.4 10.1 %all-to-all-done.2 = bf16[32,8,896]{2,1,0:T(8,128)(2,1)} async-done(((bf16[32,8,896]{2,1,0:T(8,128)(2,1)}), bf16[32,8,896]{2,1,0:T(8,128)(2,1)}, u32[]{:S(2)}, u32[]{:S(2)}) %all-to-all-start.2) | async-done | bytes 458784 | tf_op jit(solution)/shard_map/sums/all_to_all | solution.py:350
  129.5 1.1 reduce_sum.60
  130.6 0.6 copy.15
  (30 shorter events, 0.2 us)
Async XLA Ops:
  0.6 15.2 %copy-start.7 = (bf16[2,1,576]{2,0,1:T(2,128)(2,1)S(1)}, bf16[2,1,576]{2,0,1:T(2,128)(2,1)}, u32[]{:S(2)}) copy-start(bf16[2,1,576]{2,0,1:T(2,128)(2,1)} %param.14) | copy-start | bytes 6916
  0.6 21.1 %collective-permute-start.13 = (bf16[8,576,128]{2,1,0:T(8,128)(2,1)}, bf16[8,576,128]{2,1,0:T(8,128)(2,1)S(1)}, u32[]{:S(2)}, u32[]{:S(2)}) collective-permute-start(bf16[8,576,128]{2,1,0:T(8,128)(2,1)} %bitcast.65), channel_id=1, source_target_pairs={{0,128},{128,0},{1,129},{129,1},{2,130},{130,2},{3,131},{131,3},{4... | collective-permute-start | bytes 3538952 | tf_op jit(solution)/shard_map/pages/ppermute | solution.py:23
  2.4 29.7 %all-to-all-start = ((bf16[32,8,1024]{2,1,0:T(8,128)(2,1)}), bf16[32,8,1024]{2,1,0:T(8,128)(2,1)S(1)}, u32[]{:S(2)}, u32[]{:S(2)}) async-start(bf16[32,8,1024]{2,1,0:T(8,128)(2,1)} %token_.1), calls=%async_computation | async-start | bytes 1048576 | tf_op jit(solution)/shard_map/tokens/all_to_all | solution.py:250
  13.8 8.0 %collective-permute-start.12 = (s32[1,128]{1,0:T(1,128)}, s32[1,128]{1,0:T(1,128)S(1)}, u32[]{:S(2)}, u32[]{:S(2)}) collective-permute-start(s32[1,128]{1,0:T(1,128)} %bitcast.66), channel_id=1, source_target_pairs={{0,128},{128,0},{1,129},{129,1},{2,130},{130,2},{3,131},{131,3},{4... | collective-permute-start | bytes 1544 | tf_op jit(solution)/shard_map/pages/ppermute | solution.py:23
  15.2 6.5 %copy-start = (bf16[2,1,128,576]{3,2,0,1:T(8,128)(2,1)}, bf16[2,1,128,576]{3,2,0,1:T(8,128)(2,1)S(1)}, u32[]{:S(2)}) copy-start(bf16[2,1,128,576]{3,2,0,1:T(8,128)(2,1)S(1)} %copy.13) | copy-start | bytes 884740
  15.9 1.7 %copy-start.3 = (bf16[1,2048,576]{1,2,0:T(8,128)(2,1)S(1)}, bf16[1,2048,576]{1,2,0:T(8,128)(2,1)}, u32[]{:S(2)}) copy-start(bf16[1,2048,576]{1,2,0:T(8,128)(2,1)} %param.15) | copy-start | bytes 7077892
  21.8 10.4 %copy-start.1 = (f32[256,512]{1,0:T(8,128)}, f32[256,512]{1,0:T(8,128)S(1)}, u32[]{:S(2)}) copy-start(f32[256,512]{1,0:T(8,128)S(1)} %get-tuple-element.193.partial_ref.acc_in_ref) | copy-start | bytes 1572868
  34.7 11.7 %collective-permute-start.14 = (bf16[32,7296]{1,0:T(8,128)(2,1)}, bf16[32,7296]{1,0:T(8,128)(2,1)}, u32[]{:S(2)}, u32[]{:S(2)}) collective-permute-start(bf16[32,7296]{1,0:T(8,128)(2,1)} %unfold.1), channel_id=1, source_target_pairs={{0,4},{4,8},{8,12},{12,0},{1,5},{5,9},{9,13},{13,1},{2,6},{6,10},{... | collective-permute-start | bytes 1400840 | tf_op jit(solution)/shard_map/tokens/ppermute | solution.py:240
  34.9 13.7 %collective-permute-start.15 = (bf16[32,7296]{1,0:T(8,128)(2,1)}, bf16[32,7296]{1,0:T(8,128)(2,1)}, u32[]{:S(2)}, u32[]{:S(2)}) collective-permute-start(bf16[32,7296]{1,0:T(8,128)(2,1)} %unfold.1), channel_id=1, source_target_pairs={{0,12},{4,0},{8,4},{12,8},{1,13},{5,1},{9,5},{13,9},{2,14},{6,2},{... | collective-permute-start | bytes 1400840 | tf_op jit(solution)/shard_map/tokens/ppermute | solution.py:240
  36.7 67.4 %all-to-all-start.1 = ((bf16[128,8,1152]{2,1,0:T(8,128)(2,1)}), bf16[128,8,1152]{2,1,0:T(8,128)(2,1)S(1)}, u32[]{:S(2)}, u32[]{:S(2)}) async-start(bf16[128,8,1152]{2,1,0:T(8,128)(2,1)} %bitcast.5.buffer_ref), calls=%async_computation.1 | async-start | bytes 4718592 | tf_op jit(solution)/shard_map/pages/all_to_all | solution.py:321
  50.4 11.3 %collective-permute-start.2 = (bf16[16,7296]{1,0:T(8,128)(2,1)S(1)}, bf16[16,7296]{1,0:T(8,128)(2,1)S(1)}, u32[]{:S(2)}, u32[]{:S(2)}) collective-permute-start(bf16[16,7296]{1,0:T(8,128)(2,1)S(1)} %slice.282), channel_id=1, source_target_pairs={{0,4},{4,8},{8,12},{12,0},{1,5},{5,9},{9,13},{13,1},{2,6},{6,10},{... | collective-permute-start | bytes 700424 | tf_op jit(solution)/shard_map/experts/while/body/ppermute | solution.py:240
  51.5 12.2 %copy-start.4 = (bf16[1,7168,256]{2,1,0:T(8,128)(2,1)S(1)}, bf16[1,7168,256]{2,1,0:T(8,128)(2,1)}, u32[]{:S(2)}) copy-start(bf16[1,7168,256]{2,1,0:T(8,128)(2,1)} %get-tuple-element.343) | copy-start | bytes 11010052 | tf_op jit(solution)/shard_map/experts/while
  51.5 10.2 %collective-permute-start.3 = (bf16[16,7296]{1,0:T(8,128)(2,1)S(1)}, bf16[16,7296]{1,0:T(8,128)(2,1)S(1)}, u32[]{:S(2)}, u32[]{:S(2)}) collective-permute-start(bf16[16,7296]{1,0:T(8,128)(2,1)S(1)} %slice.283), channel_id=1, source_target_pairs={{0,12},{4,0},{8,4},{12,8},{1,13},{5,1},{9,5},{13,9},{2,14},{6,2},{... | collective-permute-start | bytes 700424 | tf_op jit(solution)/shard_map/experts/while/body/ppermute | solution.py:240
  61.8 1.9 %collective-permute-start.4 = (bf16[32,7296]{1,0:T(8,128)(2,1)S(1)}, bf16[32,7296]{1,0:T(8,128)(2,1)S(1)}, u32[]{:S(2)}, u32[]{:S(2)}) collective-permute-start(bf16[32,7296]{1,0:T(8,128)(2,1)S(1)} %constant_dynamic-update-slice_fusion.14), channel_id=1, source_target_pairs={{0,128},{128,0},{1,129},{129,1},{2,130},{130,2},{3,131},{131,3},{4... | collective-permute-start | bytes 1400840 | tf_op jit(solution)/shard_map/experts/while/body/ppermute | solution.py:23
  62.9 4.9 %collective-permute-start = (bf16[96,7296]{1,0:T(8,128)(2,1)S(1)}, bf16[96,7296]{1,0:T(8,128)(2,1)S(1)}, u32[]{:S(2)}, u32[]{:S(2)}) collective-permute-start(bf16[96,7296]{1,0:T(8,128)(2,1)S(1)} %constant_dynamic-update-slice_fusion.12), channel_id=1, source_target_pairs={{0,128},{128,0},{1,129},{129,1},{2,130},{130,2},{3,131},{131,3},{4... | collective-permute-start | bytes 4202504 | tf_op jit(solution)/shard_map/experts/while/body/ppermute | solution.py:23
  63.7 1.5 %copy-start.5 = (bf16[1,128,7168]{2,1,0:T(8,128)(2,1)S(1)}, bf16[1,128,7168]{2,1,0:T(8,128)(2,1)}, u32[]{:S(2)}) copy-start(bf16[1,128,7168]{2,1,0:T(8,128)(2,1)} %get-tuple-element.344) | copy-start | bytes 5505028 | tf_op jit(solution)/shard_map/experts/while
  65.6 1.9 %collective-permute-start.5 = (bf16[32,7168]{1,0:T(8,128)(2,1)S(1)}, bf16[32,7168]{1,0:T(8,128)(2,1)S(1)}, u32[]{:S(2)}, u32[]{:S(2)}) collective-permute-start(bf16[32,7168]{1,0:T(8,128)(2,1)S(1)} %multiply_convert_fusion.5), channel_id=1, source_target_pairs={{0,128},{128,0},{1,129},{129,1},{2,130},{130,2},{3,131},{131,3},{4... | collective-permute-start | bytes 1376264 | tf_op jit(solution)/shard_map/experts/while/body/ppermute | solution.py:23
  69.3 3.6 %collective-permute-start.1 = (bf16[96,7168]{1,0:T(8,128)(2,1)S(1)}, bf16[96,7168]{1,0:T(8,128)(2,1)S(1)}, u32[]{:S(2)}, u32[]{:S(2)}) collective-permute-start(bf16[96,7168]{1,0:T(8,128)(2,1)S(1)} %multiply_convert_fusion.4), channel_id=1, source_target_pairs={{0,128},{128,0},{1,129},{129,1},{2,130},{130,2},{3,131},{131,3},{4... | collective-permute-start | bytes 4128776 | tf_op jit(solution)/shard_map/experts/while/body/ppermute | solution.py:23
  69.6 12.6 %collective-permute-start.6 = (bf16[16,7168]{1,0:T(8,128)(2,1)S(1)}, bf16[16,7168]{1,0:T(8,128)(2,1)S(1)}, u32[]{:S(2)}, u32[]{:S(2)}) collective-permute-start(bf16[16,7168]{1,0:T(8,128)(2,1)S(1)} %get-tuple-element.310), channel_id=1, source_target_pairs={{0,12},{4,0},{8,4},{12,8},{1,13},{5,1},{9,5},{13,9},{2,14},{6,2},{... | collective-permute-start | bytes 688136 | tf_op jit(solution)/shard_map/experts/while/body/ppermute | solution.py:240
  70.2 12.7 %collective-permute-start.7 = (bf16[16,7168]{1,0:T(8,128)(2,1)S(1)}, bf16[16,7168]{1,0:T(8,128)(2,1)S(1)}, u32[]{:S(2)}, u32[]{:S(2)}) collective-permute-start(bf16[16,7168]{1,0:T(8,128)(2,1)S(1)} %get-tuple-element.311), channel_id=1, source_target_pairs={{0,4},{4,8},{8,12},{12,0},{1,5},{5,9},{9,13},{13,1},{2,6},{6,10},{... | collective-permute-start | bytes 688136 | tf_op jit(solution)/shard_map/experts/while/body/ppermute | solution.py:240
  73.5 14.3 %copy-start.6 = (f32[96,7168]{1,0:T(8,128)}, f32[96,7168]{1,0:T(8,128)S(1)}, u32[]{:S(2)}) copy-start(f32[96,7168]{1,0:T(8,128)S(1)} %get-tuple-element.307) | copy-start | bytes 8257540 | tf_op jit(solution)/shard_map/experts/while
  83.7 14.4 %collective-permute-start.11 = (bf16[16,7168]{1,0:T(8,128)(2,1)}, bf16[16,7168]{1,0:T(8,128)(2,1)S(1)}, u32[]{:S(2)}, u32[]{:S(2)}) collective-permute-start(bf16[16,7168]{1,0:T(8,128)(2,1)} %get-tuple-element.316), channel_id=1, source_target_pairs={{0,12},{4,0},{8,4},{12,8},{1,13},{5,1},{9,5},{13,9},{2,14},{6,2},{... | collective-permute-start | bytes 688136 | tf_op jit(solution)/shard_map/experts/while/body/ppermute | solution.py:240
  84.5 13.7 %collective-permute-start.8 = (bf16[16,7168]{1,0:T(8,128)(2,1)}, bf16[16,7168]{1,0:T(8,128)(2,1)S(1)}, u32[]{:S(2)}, u32[]{:S(2)}) collective-permute-start(bf16[16,7168]{1,0:T(8,128)(2,1)} %get-tuple-element.312), channel_id=1, source_target_pairs={{0,4},{4,8},{8,12},{12,0},{1,5},{5,9},{9,13},{13,1},{2,6},{6,10},{... | collective-permute-start | bytes 688136 | tf_op jit(solution)/shard_map/experts/while/body/ppermute | solution.py:240
  87.8 15.1 %collective-permute-start.10 = (bf16[16,7168]{1,0:T(8,128)(2,1)}, bf16[16,7168]{1,0:T(8,128)(2,1)S(1)}, u32[]{:S(2)}, u32[]{:S(2)}) collective-permute-start(bf16[16,7168]{1,0:T(8,128)(2,1)} %get-tuple-element.315), channel_id=1, source_target_pairs={{0,12},{4,0},{8,4},{12,8},{1,13},{5,1},{9,5},{13,9},{2,14},{6,2},{... | collective-permute-start | bytes 688136 | tf_op jit(solution)/shard_map/experts/while/body/ppermute | solution.py:240
  87.8 15.1 %collective-permute-start.9 = (bf16[16,7168]{1,0:T(8,128)(2,1)}, bf16[16,7168]{1,0:T(8,128)(2,1)S(1)}, u32[]{:S(2)}, u32[]{:S(2)}) collective-permute-start(bf16[16,7168]{1,0:T(8,128)(2,1)} %get-tuple-element.314), channel_id=1, source_target_pairs={{0,4},{4,8},{8,12},{12,0},{1,5},{5,9},{9,13},{13,1},{2,6},{6,10},{... | collective-permute-start | bytes 688136 | tf_op jit(solution)/shard_map/experts/while/body/ppermute | solution.py:240
  104.2 10.8 %copy-start.2 = (f32[256,512]{1,0:T(8,128)S(1)}, f32[256,512]{1,0:T(8,128)}, u32[]{:S(2)}) copy-start(f32[256,512]{1,0:T(8,128)} %copy-done.1) | copy-start | bytes 1572868
  104.2 25.3 %all-to-all-start.2 = ((bf16[32,8,896]{2,1,0:T(8,128)(2,1)}), bf16[32,8,896]{2,1,0:T(8,128)(2,1)}, u32[]{:S(2)}, u32[]{:S(2)}) async-start(bf16[32,8,896]{2,1,0:T(8,128)(2,1)} %get-tuple-element.198), calls=%async_computation.2 | async-start | bytes 917504 | tf_op jit(solution)/shard_map/sums/all_to_all | solution.py:350
